TPU v7x, 32 devices: a whole 2x2x4 slice. The times are simulated.
32 devices in a mesh: chan: 4 (over x, core), blk: 8 (over z, y).
Axes of the slice: x: 2, y: 2, z: 4, core: 2. Of those that a mesh axis runs over, the one named last changes fastest.
Arguments:
- voltages: bfloat16 [64, 262144], P('blk', 'chan'), may hold values from -6 to 6
- fir_taps: float32 [8, 4096], replicated, may hold values from -2.1 to 2.1
Outputs:
- visibilities: float32 [2, 64, 64, 2048], P(None, 'blk', None, 'chan')
All inputs are finite; a program needn't handle non-finite values.
Results may differ from a plain program's by a relative error of at most 0.0036.
Values may be sent and summed in bfloat16 or wider, within the bound.
A program may use at most 192 MiB of HBM per device.

v0:
```python
import math

import jax
import jax.numpy as jnp
from jax import lax
from jax.sharding import PartitionSpec as P

TAPS = 8
L = 4096
C = 2048


def shifted(value, axis, steps):
    count = lax.axis_size(axis)
    leading, last = (max(0, -steps), min(count, count - steps))
    return lax.ppermute(value, axis, [(source, source + steps) for source in range(leading, last)])


def dft_table(first_channel, channel_count, length):
    channel_ids = first_channel + jnp.arange(channel_count, dtype=jnp.int32)
    sample_ids = jnp.arange(length, dtype=jnp.int32)
    phase_index = sample_ids[:, None] * channel_ids[None, :] % length
    angles = phase_index.astype(jnp.float32) * (2.0 * math.pi / length)
    normaliser = 1.0 / math.sqrt(length)
    return jnp.concatenate([jnp.cos(angles) * normaliser, -jnp.sin(angles) * normaliser], axis=1)


def correlate_pair(left_block, right_block, inverse_count):
    gram_terms = jnp.einsum(
        "itpc,jtqc->ipjqc", left_block, right_block, preferred_element_type=jnp.float32
    )
    real_part = gram_terms[:, 0, :, 0] + gram_terms[:, 1, :, 1]
    imag_part = gram_terms[:, 1, :, 0] - gram_terms[:, 0, :, 1]
    return jnp.stack([real_part, imag_part]) * inverse_count


def on_device(voltages, fir_taps):
    feed_count = voltages.shape[0]
    frame_count = voltages.shape[1] // L
    own_frames = voltages.reshape(feed_count, frame_count, L)
    last_frames = own_frames[:, frame_count - (TAPS - 1) :, :]
    earlier = shifted(last_frames, "chan", 1)
    extended = jnp.concatenate([earlier, own_frames], axis=1)
    filtered = jnp.zeros((feed_count, frame_count, L), jnp.float32)
    for tap_index in range(TAPS):
        filtered = filtered + fir_taps[tap_index][None, None, :] * extended[
            :, tap_index : tap_index + frame_count, :
        ].astype(jnp.float32)
    frame_rows = filtered.reshape(feed_count * frame_count, L)
    block_width = min(C, 512)
    pieces = []
    for first_channel in range(0, C, block_width):
        cos_sin_table = dft_table(first_channel, block_width, L)
        product = jnp.dot(
            frame_rows,
            cos_sin_table,
            precision=lax.Precision.HIGHEST,
            preferred_element_type=jnp.float32,
        )
        pieces.append(product.reshape(feed_count * frame_count, 2, block_width))
    spectra = (
        jnp.concatenate(pieces, axis=2).astype(jnp.bfloat16).reshape(feed_count, frame_count, 2, C)
    )
    own_block = lax.all_to_all(spectra, "chan", split_axis=3, concat_axis=1, tiled=True)
    inverse_count = 1.0 / own_block.shape[1]
    return correlate_pair(
        own_block, lax.all_gather(own_block, "blk", axis=0, tiled=True), inverse_count
    )


def solution(mesh):
    placed = (P("blk", "chan"), P())
    return jax.shard_map(
        on_device,
        mesh=mesh,
        in_specs=placed,
        out_specs=P(None, "blk", None, "chan"),
        check_vma=False,
    )
```

profile of v0, /device:TPU:0, one launch (start us, length us, event | category | flops | bytes accessed | tf_op | source)
XLA Modules:
  0.0 612.7 jit_solution(5157199918161761279)
XLA Ops:
  6.5 0.0 all-gather.2.cloned.1.call-start
  6.5 1.8 copy.39
  8.3 0.1 slice.80
  8.5 3.2 collective-permute-start
  11.7 33.0 %negate_multiply_fusion.3 = (f32[4096,512]{0,1:T(8,128)S(1)}, f32[4096,512]{0,1:T(8,128)S(1)}) fusion(), kind=kLoop, calls=%fused_computation.42 | loop fusion | flops 35651584 | bytes 16777216 | tf_op jit(solution)/shard_map/mul | solution.py:25
  44.7 0.0 copy-done.6
  44.7 0.1 fusion.54
  44.8 33.5 %cosine_multiply_fusion = (f32[4096,512]{0,1:T(8,128)S(1)}, f32[4096,512]{0,1:T(8,128)S(1)}) fusion(s32[512]{0:T(512)S(1)} %iota_add_fusion), kind=kLoop, calls=%fused_computation.31 | loop fusion | flops 35651584 | bytes 16779264 | tf_op jit(solution)/shard_map/mul | solution.py:25
  78.3 37.2 %cosine_multiply_fusion.1 = (f32[4096,512]{0,1:T(8,128)}, f32[4096,512]{0,1:T(8,128)}) fusion(s32[512]{0:T(512)S(1)} %iota_add_fusion.1), kind=kLoop, calls=%fused_computation.35 | loop fusion | flops 35651584 | bytes 16779264 | tf_op jit(solution)/shard_map/mul | solution.py:25
  115.5 37.2 %cosine_multiply_fusion.2 = (f32[4096,512]{0,1:T(8,128)}, f32[4096,512]{0,1:T(8,128)}) fusion(s32[512]{0:T(512)S(1)} %iota_add_fusion.2), kind=kLoop, calls=%fused_computation.39 | loop fusion | flops 35651584 | bytes 16779264 | tf_op jit(solution)/shard_map/mul | solution.py:25
  152.8 6.4 %pad_maximum_fusion.3 = f32[4096,1024]{0,1:T(8,128)} fusion(f32[4096,512]{0,1:T(8,128)S(1)} %get-tuple-element.20, f32[4096,512]{0,1:T(8,128)S(1)} %get-tuple-element.19), kind=kLoop, calls=%fused_computation.3 | loop fusion | flops 4194304 | bytes 33554432 | tf_op jit(solution)/shard_map/concatenate | solution.py:25
  159.1 13.7 %pad_maximum_fusion.2 = f32[4096,1024]{0,1:T(8,128)} fusion(f32[4096,512]{0,1:T(8,128)} %get-tuple-element.18, f32[4096,512]{0,1:T(8,128)} %get-tuple-element.17), kind=kLoop, calls=%fused_computation.2 | loop fusion | flops 4194304 | bytes 33554432 | tf_op jit(solution)/shard_map/concatenate | solution.py:25
  172.9 0.0 copy-done
  172.9 2.7 copy-done.1
  175.6 6.8 %pad_maximum_fusion.1 = f32[4096,1024]{0,1:T(8,128)} fusion(f32[4096,512]{0,1:T(8,128)S(1)} %copy-done.1, f32[4096,512]{0,1:T(8,128)S(1)} %copy-done), kind=kLoop, calls=%fused_computation.1 | loop fusion | flops 4194304 | bytes 33554432 | tf_op jit(solution)/shard_map/concatenate | solution.py:25
  182.4 6.4 %pad_maximum_fusion = f32[4096,1024]{0,1:T(8,128)} fusion(f32[4096,512]{0,1:T(8,128)S(1)} %get-tuple-element.21, f32[4096,512]{0,1:T(8,128)S(1)} %get-tuple-element.22), kind=kLoop, calls=%fused_computation | loop fusion | flops 4194304 | bytes 33554432 | tf_op jit(solution)/shard_map/concatenate | solution.py:25
  188.8 0.0 collective-permute-done
  188.8 5.6 multiply_add_fusion
  194.5 0.0 copy-start.2
  194.5 0.0 slice-start.1
  194.5 0.0 slice-start.2
  194.5 0.0 slice-start.3
  194.5 22.3 %fusion.43 = bf16[8,16,2,512]{3,1,2,0:T(8,128)(2,1)} fusion(f32[2,512,4096,1]{2,1,0,3:T(8,128)} %bitcast.73, f32[8,16,4096]{2,1,0:T(8,128)S(1)} %multiply_add_fusion), kind=kOutput, calls=%fused_computation.75 | convolution fusion | flops 6442582016 | bytes 19136512 | tf_op jit(solution)/shard_map/dot_general | solution.py:54
  216.8 0.0 copy-done.2
  216.8 0.0 slice-done
  216.8 0.0 copy-start.3
  216.8 0.0 slice-start.4
  216.9 0.0 slice-start.5
  216.9 20.2 %fusion.40 = bf16[8,16,2,512]{3,1,2,0:T(8,128)(2,1)} fusion(f32[2,512,4096,1]{2,1,0,3:T(8,128)S(1)} %bitcast.76, f32[8,16,4096]{2,1,0:T(8,128)} %copy-done.2), kind=kOutput, calls=%fused_computation.74 | convolution fusion | flops 6442582016 | bytes 19136512 | tf_op jit(solution)/shard_map/dot_general | solution.py:54
  237.1 20.8 %fusion.37 = bf16[8,16,2,512]{3,1,2,0:T(8,128)(2,1)S(1)} fusion(f32[2,512,4096,1]{2,1,0,3:T(8,128)} %bitcast.77, f32[8,16,4096]{2,1,0:T(8,128)S(1)} %copy-done.3), kind=kOutput, calls=%fused_computation.73 | convolution fusion | flops 6442582016 | bytes 19136512 | tf_op jit(solution)/shard_map/dot_general | solution.py:54
  257.9 17.6 %fusion.34 = bf16[8,16,2,512]{3,1,2,0:T(8,128)(2,1)S(1)} fusion(f32[2,512,4096,1]{2,1,0,3:T(8,128)S(1)} %bitcast.80, f32[8,16,4096]{2,1,0:T(8,128)S(1)} %copy-done.3), kind=kOutput, calls=%fused_computation.72 | convolution fusion | flops 6442582016 | bytes 19136512 | tf_op jit(solution)/shard_map/dot_general | solution.py:54
  275.5 0.0 copy-done.4
  275.5 0.0 copy-done.5
  275.5 0.1 pad_maximum_fusion.5
  275.6 14.8 %copy.42 = bf16[8,16,2,2048]{1,2,0,3:T(2,128)(2,1)} copy(bf16[8,16,2,2048]{3,1,2,0:T(8,128)(2,1)S(1)} %pad_maximum_fusion.5) | data formatting | bytes 2097152 | tf_op jit(solution)/shard_map/concatenate | solution.py:62
  290.4 10.2 %reshape.89 = bf16[4,2,65536]{2,1,0:T(2,128)(2,1)S(1)} reshape(bf16[2048,8,2,16]{3,2,1,0:T(2,128)(2,1)} %bitcast.70) | data formatting | bytes 2097152
  300.6 17.4 %all_to_all.18 = bf16[4,2,65536]{2,1,0:T(2,128)(2,1)S(1)} all-to-all(bf16[4,2,65536]{2,1,0:T(2,128)(2,1)S(1)} %reshape.89), channel_id=1, replica_groups=mesh['chan'=4,'blk'=8] {'chan'}, dimensions={0} | all-to-all | bytes 2097152 | tf_op jit(solution)/shard_map/all_to_all | solution.py:64
  318.0 7.2 %reshape.90 = bf16[2048,8,2,16]{3,2,1,0:T(2,128)(2,1)} reshape(bf16[4,2,65536]{2,1,0:T(2,128)(2,1)S(1)} %all_to_all.18) | data formatting | bytes 2097152
  325.2 19.1 %copy.51 = bf16[8,16,2,4,512]{4,3,1,2,0:T(4,128)(2,1)S(1)} copy(bf16[8,16,2,4,512]{1,2,0,4,3:T(2,128)(2,1)} %bitcast.71) | data formatting | bytes 2097152 | tf_op jit(solution)/shard_map/all_to_all | solution.py:64
  344.3 0.2 copy.44
  344.5 2.8 copy.45
  347.4 0.0 all-gather.2.cloned.1.call-update
  347.4 2.0 copy.50
  349.4 226.6 %all-gather.2.cloned.1.call-done = bf16[64,64,2,512]{1,0,2,3:T(8,128)(2,1)} async-done(((bf16[8,64,2,512]{1,0,2,3:T(8,128)(2,1)}), bf16[64,64,2,512]{1,0,2,3:T(8,128)(2,1)}) %all-gather.2.cloned.1.call-update) | async-done | bytes 8388624 | tf_op jit(solution)/shard_map/all_gather | solution.py:67
  576.0 18.6 %fusion = f32[512,64,2,8,2]{1,3,4,2,0:T(8,128)} fusion(bf16[8,64,2,512,1]{1,0,2,4,3:T(8,128)(2,1)S(1)} %copy.50, bf16[64,64,2,512]{1,0,2,3:T(8,128)(2,1)} %all-gather.2.cloned.1.call-done), kind=kOutput, calls=%fused_computation.4 | convolution fusion | flops 134217728 | bytes 13631488 | tf_op jit(solution)/shard_map/itpc,jtqc->ipjqc/dot_general | solution.py:29
  594.6 6.8 %copy.47 = f32[512,64,2,8,2]{0,1,3,2,4:T(8,128)} copy(f32[512,64,2,8,2]{1,3,4,2,0:T(8,128)} %fusion) | data formatting | bytes 8388608 | tf_op jit(solution)/shard_map/itpc,jtqc->ipjqc/dot_general | solution.py:29
  601.4 2.6 fusion.53
  604.1 1.6 maximum_multiply_fusion
  (21 shorter events, 0.0 us)
Async XLA Ops:
  6.5 569.5 %all-gather.2.cloned.1.call-start = ((), (), s32[]{:S(2)}) async-start(), calls=%async_computation.1 | async-start | bytes 18874368 | tf_op jit(solution)/shard_map/all_gather | solution.py:67
  8.5 180.3 %collective-permute-start = (bf16[8,7,4096]{2,1,0:T(8,128)(2,1)S(1)}, bf16[8,7,4096]{2,1,0:T(8,128)(2,1)}, u32[]{:S(2)}, u32[]{:S(2)}) collective-permute-start(bf16[8,7,4096]{2,1,0:T(8,128)(2,1)S(1)} %slice.80), channel_id=1, source_target_pairs={{0,8},{8,16},{16,24},{1,9},{9,17},{17,25},{2,10},{10,18},{18,26},{... | collective-permute-start | bytes 1376264 | tf_op jit(solution)/shard_map/ppermute | solution.py:16
  11.7 33.0 %copy-start.6 = (f32[8,4096]{1,0:T(8,128)S(1)}, f32[8,4096]{1,0:T(8,128)}, u32[]{:S(2)}) copy-start(f32[8,4096]{1,0:T(8,128)} %param.3) | copy-start | bytes 393220
  159.1 13.7 %copy-start = (f32[4096,512]{0,1:T(8,128)S(1)}, f32[4096,512]{0,1:T(8,128)}, u32[]{:S(2)}) copy-start(f32[4096,512]{0,1:T(8,128)} %get-tuple-element.15) | copy-start | bytes 25165828
  159.1 16.5 %copy-start.1 = (f32[4096,512]{0,1:T(8,128)S(1)}, f32[4096,512]{0,1:T(8,128)}, u32[]{:S(2)}) copy-start(f32[4096,512]{0,1:T(8,128)} %get-tuple-element.16) | copy-start | bytes 25165828
  188.8 28.0 %slice-start = ((s8[16777216]{0:T(1024)(128)(4,1)}), s8[4194304]{0:T(1024)(128)(4,1)S(1)}, s32[]{:S(2)}) async-start(s8[16777216]{0:T(1024)(128)(4,1)} %bitcast.74), calls=%async_computation.2 | async-start | bytes 8388608
  194.5 22.3 %copy-start.2 = (f32[8,16,4096]{2,1,0:T(8,128)}, f32[8,16,4096]{2,1,0:T(8,128)S(1)}, u32[]{:S(2)}) copy-start(f32[8,16,4096]{2,1,0:T(8,128)S(1)} %multiply_add_fusion) | copy-start | bytes 6291460
  194.5 22.3 %slice-start.1 = ((s8[16777216]{0:T(1024)(128)(4,1)}), s8[4194304]{0:T(1024)(128)(4,1)S(1)}, s32[]{:S(2)}) async-start(s8[16777216]{0:T(1024)(128)(4,1)} %bitcast.74), calls=%async_computation.3 | async-start | bytes 8388608
  194.5 22.3 %slice-start.2 = ((s8[16777216]{0:T(1024)(128)(4,1)}), s8[4194304]{0:T(1024)(128)(4,1)S(1)}, s32[]{:S(2)}) async-start(s8[16777216]{0:T(1024)(128)(4,1)} %bitcast.74), calls=%async_computation.4 | async-start | bytes 8388608
  194.5 22.3 %slice-start.3 = ((s8[16777216]{0:T(1024)(128)(4,1)}), s8[4194304]{0:T(1024)(128)(4,1)S(1)}, s32[]{:S(2)}) async-start(s8[16777216]{0:T(1024)(128)(4,1)} %bitcast.74), calls=%async_computation.5 | async-start | bytes 8388608
  216.8 20.2 %copy-start.3 = (f32[8,16,4096]{2,1,0:T(8,128)S(1)}, f32[8,16,4096]{2,1,0:T(8,128)}, u32[]{:S(2)}) copy-start(f32[8,16,4096]{2,1,0:T(8,128)} %copy-done.2) | copy-start | bytes 6291460
  216.8 41.0 %slice-start.4 = ((s8[16777216]{0:T(1024)(128)(4,1)}), s8[4194304]{0:T(1024)(128)(4,1)S(1)}, s32[]{:S(2)}) async-start(s8[16777216]{0:T(1024)(128)(4,1)} %bitcast.78), calls=%async_computation.6 | async-start | bytes 8388608
  216.9 41.0 %slice-start.5 = ((s8[16777216]{0:T(1024)(128)(4,1)}), s8[4194304]{0:T(1024)(128)(4,1)S(1)}, s32[]{:S(2)}) async-start(s8[16777216]{0:T(1024)(128)(4,1)} %bitcast.78), calls=%async_computation.7 | async-start | bytes 8388608
  237.1 20.8 %slice-start.6 = ((s8[16777216]{0:T(1024)(128)(4,1)}), s8[4194304]{0:T(1024)(128)(4,1)S(1)}, s32[]{:S(2)}) async-start(s8[16777216]{0:T(1024)(128)(4,1)} %bitcast.78), calls=%async_computation.8 | async-start | bytes 8388608
  237.1 20.8 %slice-start.7 = ((s8[16777216]{0:T(1024)(128)(4,1)}), s8[4194304]{0:T(1024)(128)(4,1)S(1)}, s32[]{:S(2)}) async-start(s8[16777216]{0:T(1024)(128)(4,1)} %bitcast.78), calls=%async_computation.9 | async-start | bytes 8388608
  257.9 17.6 %copy-start.4 = (bf16[8,16,2,512]{3,1,2,0:T(8,128)(2,1)S(1)}, bf16[8,16,2,512]{3,1,2,0:T(8,128)(2,1)}, u32[]{:S(2)}) copy-start(bf16[8,16,2,512]{3,1,2,0:T(8,128)(2,1)} %fusion.43) | copy-start | bytes 786436
  257.9 17.6 %copy-start.5 = (bf16[8,16,2,512]{3,1,2,0:T(8,128)(2,1)S(1)}, bf16[8,16,2,512]{3,1,2,0:T(8,128)(2,1)}, u32[]{:S(2)}) copy-start(bf16[8,16,2,512]{3,1,2,0:T(8,128)(2,1)} %fusion.40) | copy-start | bytes 786436
Sparse Core Ops, SparseCore 0:
  347.5 228.4 all-gather.1
where the time goes:
time: 620 us; the launch traced here: 613 us
  waiting for transfers between devices  227 us (37%)
  other arithmetic  184 us (30%)
  matrix products  99.4 us (16%)
  local copies, waits for them, and re-layouts  68 us (11%)
  blocking collectives  17.4 us (3%)
  between operations  13.9 us (2%)
    all_gather x1, waiting for transfers between devices, on_device(): lax.all_gather(own_block, 'blk', axis=0, tiled=True)  227 us
    mul x3, other arithmetic, dft_table(): jnp.cos(angles) * normaliser  108 us
    dot_general x4, matrix products, on_device(): jnp.dot(frame_rows, cos_sin_table, precision=lax.Precision.HIGHEST, prefe...  80.8 us
    concatenate x4, other arithmetic, dft_table(): jnp.concatenate([jnp.cos(angles) * normaliser, -jnp.sin(angles) * normali...  33.3 us
    mul x1, other arithmetic, dft_table(): -jnp.sin(angles) * normaliser  33 us
    all_to_all x4, local copies, waits for them, and re-layouts, on_device(): lax.all_to_all(spectra, 'chan', split_axis=3, concat_axis=1, tiled=True)  24.2 us
    unnamed x32, local copies, waits for them, and re-layouts  20.2 us
    dot_general x1, matrix products, correlate_pair(): jnp.einsum('itpc,jtqc->ipjqc', left_block, right_block, preferred_element...  18.6 us
  transfers between devices with their start and end apart: 2, of which 1 were waited for; matrix products, arithmetic and copies ran while one was open for 29% of the time, Pallas kernels for 0%

commit v1 on v0

v1 whole, which is shorter than its diff:
```python
import functools
import math

import jax
import jax.numpy as jnp
import numpy as np
from jax import lax
from jax.experimental import pallas as pl
from jax.experimental.pallas import tpu as pltpu
from jax.sharding import PartitionSpec as P

TAPS = 8
L = 4096
C = 2048
N2 = 128
N1 = L // N2
HALF = C // N1
VMEM = 56 * 1024 * 1024


def tables():
    n2 = np.arange(N2)
    angle = 2.0 * np.pi * (np.arange(N1)[:, None] * n2[None, :] % L) / L
    twiddle = np.stack([np.cos(angle), np.sin(angle)]).astype(np.float32)
    angle = 2.0 * np.pi * (np.arange(HALF)[:, None] * n2[None, :] % N2) / N2
    cos, sin = np.cos(angle) / math.sqrt(L), np.sin(angle) / math.sqrt(L)
    matrix = np.block([[cos, sin], [-sin, cos]])
    high = matrix.astype(jnp.bfloat16)
    low = (matrix - high.astype(np.float64)).astype(jnp.bfloat16)
    return twiddle, high, low


def times(scale, value):
    return None if value is None else scale * value


def plus(a, b):
    return b if a is None else a if b is None else a + b


def minus(a, b):
    return a if b is None else -b if a is None else a - b


def real_dft(values):
    n = len(values)
    if n == 1:
        return [(values[0], None)]
    half = n // 2
    even, odd = real_dft(values[0::2]), real_dft(values[1::2])
    result = [None] * (half + 1)
    for k in range(half // 2 + 1):
        (er, ei), (odr, odi) = even[k], odd[k]
        if k == 0:
            tr, ti = odr, odi
        elif 4 * k == n:
            tr, ti = odi, -odr
        else:
            c, s = math.cos(2 * math.pi * k / n), math.sin(2 * math.pi * k / n)
            tr = plus(times(c, odr), times(s, odi))
            ti = minus(times(c, odi), times(s, odr))
        result[half - k] = (minus(er, tr), minus(ti, ei))
        result[k] = (plus(er, tr), plus(ei, ti))
    return result


def fir_stage(volt, halo, taps, filtered, frames):
    @pl.loop(0, N1)
    def _(n1):
        lane = pl.multiple_of(n1 * N2, N2)
        weights = [jnp.broadcast_to(taps[t : t + 1, pl.ds(lane, N2)], (8, N2)) for t in range(TAPS)]
        window = [halo[:, pl.ds(f * L + lane, N2)].astype(jnp.float32) for f in range(TAPS - 1)]
        for f in range(frames):
            window.append(volt[:, pl.ds(f * L + lane, N2)].astype(jnp.float32))
            total = weights[0] * window[f]
            for t in range(1, TAPS):
                total = total + weights[t] * window[f + t]
            filtered[f * N1 + n1] = total


def first_stage(filtered, twiddle, turned, frames):
    @pl.loop(0, frames)
    def _(f):
        spectrum = real_dft([filtered[f * N1 + n1] for n1 in range(N1)])
        row = pl.multiple_of(f * 8, 8)
        for k1 in range(N1):
            if 2 * k1 <= N1:
                zr, zi = spectrum[k1]
            else:
                zr, zi = spectrum[N1 - k1]
                zi = -zi
            c = twiddle[0, k1 : k1 + 1, :]
            s = twiddle[1, k1 : k1 + 1, :]
            if k1 == 0:
                re, im = zr, jnp.zeros_like(zr)
            elif zi is None:
                re, im = c * zr, -(s * zr)
            else:
                re, im = c * zr + s * zi, c * zi - s * zr
            turned[k1, pl.ds(row, 8), pl.ds(0, N2)] = re
            turned[k1, pl.ds(row, 8), pl.ds(N2, N2)] = im


def second_stage(turned, high, low, ordered):
    contract = (((1,), (1,)), ((), ()))
    wh, wl = high[...], low[...]
    for k1 in range(N1):
        z = turned[k1]
        zh = z.astype(jnp.bfloat16)
        zl = (z - zh.astype(jnp.float32)).astype(jnp.bfloat16)
        out = lax.dot_general(wl, zh, contract, preferred_element_type=jnp.float32)
        out = out + lax.dot_general(wh, zl, contract, preferred_element_type=jnp.float32)
        out = out + lax.dot_general(wh, zh, contract, preferred_element_type=jnp.float32)
        for p in range(2):
            ordered[pl.ds(p * C + k1, HALF, stride=N1), :] = out[p * HALF : (p + 1) * HALF]


def spectra_kernel(frames, parts, volt, halo, taps, twiddle, high, low, out, filtered, turned, ordered):
    fir_stage(volt, halo, taps, filtered, frames)
    first_stage(filtered, twiddle, turned, frames)
    second_stage(turned, high, low, ordered)
    chn = C // parts

    @pl.loop(0, parts)
    def _(d):
        for p in range(2):
            out[d, p] = ordered[pl.ds(pl.multiple_of(p * C + d * chn, chn), chn), :].astype(jnp.bfloat16)


def regroup(groups, lane):
    count = len(groups)
    d = 1
    while d < count:
        low_side = (lane & d) == 0
        result = list(groups)
        for g in range(count):
            if g & d == 0:
                a, b = groups[g], groups[g | d]
                result[g] = jnp.where(low_side, a, pltpu.roll(b, d, 1))
                result[g | d] = jnp.where(low_side, pltpu.roll(a, 128 - d, 1), b)
        groups = result
        d *= 2
    return groups


def gather_feeds(get, blk, chan, chn, grouped):
    lane = lax.broadcasted_iota(jnp.int32, (chn, 128), 1)

    @pl.loop(0, blk)
    def _(b):
        arrays = [get(c, b, p).astype(jnp.float32) for p in range(2) for c in range(chan)]
        for feed, value in enumerate(regroup(arrays, lane)):
            row = pl.multiple_of((b * 8 + feed) * chn, chn)
            grouped[pl.ds(row, chn), :] = value


def correlate(grouped, blk, chan, chn, spectra_count, put):
    feeds = blk * 8
    lane = lax.broadcasted_iota(jnp.int32, (feeds, 128), 1)
    real_lane = (lane & chan) == 0
    contract = (((1,), (1,)), ((), ()))

    def one(ch):
        value = grouped[pl.ds(ch, feeds, stride=chn), :]
        other = jnp.where(real_lane, -pltpu.roll(value, 128 - chan, 1), pltpu.roll(value, chan, 1))
        left = value.astype(jnp.bfloat16)
        right = jnp.concatenate([left, other.astype(jnp.bfloat16)], axis=0)
        out = lax.dot_general(left, right, contract, preferred_element_type=jnp.float32)
        return out * (1.0 / spectra_count)

    @pl.loop(0, chn // 2)
    def _(h):
        first, second = one(2 * h), one(2 * h + 1)
        for b in range(blk):
            rows = jnp.concatenate([first[b * 8 : b * 8 + 8], second[b * 8 : b * 8 + 8]], axis=0)
            put(b, pl.multiple_of(h * 16, 16), rows.astype(jnp.bfloat16))


def correlate_kernel(blk, chan, chn, spectra_count, seen, out, grouped):
    gather_feeds(lambda c, b, p: seen[c * blk + b, p], blk, chan, chn, grouped)

    def put(b, row, rows):
        out[b, pl.ds(row, 16), :] = rows

    correlate(grouped, blk, chan, chn, spectra_count, put)


def finish(get, blk, chn, feeds, out, wide):
    @pl.loop(0, blk)
    def _(b):
        for first in range(0, 2 * feeds, 128):
            value = get(b, first).astype(jnp.float32)
            wide[first // 128, pl.ds(pl.multiple_of(b * chn * 8, chn * 8), chn * 8), :] = value

    piece = min(feeds, 128)
    for i in range(8):
        for block in range(0, blk * chn, 128):
            for first in range(0, 2 * feeds, 128):
                tile = wide[first // 128, pl.ds(block * 8 + i, 128, stride=8), :].T
                for at in range(0, 128, piece):
                    part, j = divmod(first + at, feeds)
                    out[part, i, pl.ds(j, piece), pl.ds(block, 128)] = tile[at : at + piece]


def finish_kernel(blk, chn, feeds, seen, out, wide):
    finish(lambda b, first: seen[b, :, first : first + 128], blk, chn, feeds, out, wide)


def whole(count):
    return [pl.BlockSpec(memory_space=pltpu.VMEM)] * count


def on_device(chan, blk, voltages, fir_taps):
    frames = voltages.shape[1] // L
    parts = chan * blk
    chn = C // parts
    feeds = blk * 8
    spectra_count = frames * chan
    twiddle, high, low = tables()
    last = voltages[:, (frames - TAPS + 1) * L :]
    halo = lax.ppermute(last, "chan", [(a, a + 1) for a in range(chan - 1)])
    params = pltpu.CompilerParams(vmem_limit_bytes=VMEM)
    spectra = pl.pallas_call(
        functools.partial(spectra_kernel, frames, parts),
        out_shape=jax.ShapeDtypeStruct((parts, 2, chn, 128), jnp.bfloat16),
        in_specs=whole(6),
        out_specs=whole(1)[0],
        scratch_shapes=[
            pltpu.VMEM((frames * N1, 8, N2), jnp.float32),
            pltpu.VMEM((N1, 8 * frames, 2 * N2), jnp.float32),
            pltpu.VMEM((2 * C, 8 * frames), jnp.float32),
        ],
        compiler_params=params,
        name="spectra",
    )(voltages, halo, fir_taps, jnp.asarray(twiddle), jnp.asarray(high), jnp.asarray(low))
    seen = lax.all_to_all(spectra, ("chan", "blk"), split_axis=0, concat_axis=0, tiled=True)
    products = pl.pallas_call(
        functools.partial(correlate_kernel, blk, chan, chn, spectra_count),
        out_shape=jax.ShapeDtypeStruct((blk, chn * 8, 2 * feeds), jnp.bfloat16),
        in_specs=whole(1),
        out_specs=whole(1)[0],
        scratch_shapes=[pltpu.VMEM((feeds * chn, 128), jnp.float32)],
        compiler_params=params,
        name="correlate",
    )(seen)
    mine = lax.all_to_all(products, "blk", split_axis=0, concat_axis=0, tiled=True)
    return pl.pallas_call(
        functools.partial(finish_kernel, blk, chn, feeds),
        out_shape=jax.ShapeDtypeStruct((2, 8, feeds, blk * chn), jnp.float32),
        in_specs=whole(1),
        out_specs=whole(1)[0],
        scratch_shapes=[pltpu.VMEM((feeds // 64, blk * chn * 8, 128), jnp.float32)],
        compiler_params=params,
        name="finish",
    )(mine)


def solution(mesh):
    chan, blk = mesh.shape["chan"], mesh.shape["blk"]
    return jax.shard_map(
        functools.partial(on_device, chan, blk),
        mesh=mesh,
        in_specs=(P("blk", "chan"), P()),
        out_specs=P(None, "blk", None, "chan"),
        check_vma=False,
    )
```

time: 620 us -> 100 us (0.16); the launches traced: 613 us -> 99.6 us
  waiting for transfers between devices: 227 us -> 1.4 us
  other arithmetic: 184 us -> 0 us
  matrix products: 99.4 us -> 0 us
  local copies, waits for them, and re-layouts: 68 us -> 1.81 us
  blocking collectives: 17.4 us -> 71.1 us
  Pallas kernels: 0 us -> 22.9 us
  between operations: 13.9 us -> 0.02 us
    all_gather x1 -> x0, waiting for transfers between devices: 227 us -> none  [on_device(): lax.all_gather(own_block, 'blk', axis=0, tiled=True)]
    mul x5 -> x0, other arithmetic: 143 us -> none  [the longest x3 108 us: dft_table(): jnp.cos(angles) * normaliser]
    dot_general x5 -> x0, matrix products: 99.4 us -> none  [the longest x4 80.8 us: on_device(): jnp.dot(frame_rows, cos_sin_table, precision=lax.Precision.HIGHEST, prefe...]
    all_to_all x1 -> x2, blocking collectives: 17.4 us -> 71.1 us  [the longest x1 41 us: on_device(): lax.all_to_all(spectra, ('chan', 'blk'), split_axis=0, concat_axis=0, til...]
    concatenate x5 -> x0, other arithmetic: 33.4 us -> none  [the longest x4 33.3 us: dft_table(): jnp.concatenate([jnp.cos(angles) * normaliser, -jnp.sin(angles) * normali...]
    all_to_all x4 -> x0, local copies, waits for them, and re-layouts: 24.2 us -> none  [on_device(): lax.all_to_all(spectra, 'chan', split_axis=3, concat_axis=1, tiled=True)]
    pallas_call x0 -> x3, Pallas kernels: none -> 22.9 us  [the longest x1 11.9 us: on_device(): pl.pallas_call(functools.partial(correlate_kernel, blk, chan, chn, spectr...]
    unnamed x32 -> x2, local copies, waits for them, and re-layouts: 20.2 us -> 0.76 us
  transfers between devices with their start and end apart: 2 -> 1, of which waited for: 1 -> 1; matrix products, arithmetic and copies ran while one was open for 29% -> 0% of each run, Pallas kernels for 0% -> 0%
where the time goes in v1:
time: 100 us; the launch traced here: 99.6 us
  blocking collectives  71.1 us (71%)
  Pallas kernels  22.9 us (23%)
  starting transfers between devices  2.39 us (2%)
  local copies, waits for them, and re-layouts  1.81 us (2%)
  waiting for transfers between devices  1.4 us (1%)
    all_to_all x1, blocking collectives, on_device(): lax.all_to_all(spectra, ('chan', 'blk'), split_axis=0, concat_axis=0, til...  41 us
    all_to_all x1, blocking collectives, on_device(): lax.all_to_all(products, 'blk', split_axis=0, concat_axis=0, tiled=True)  30.1 us
    pallas_call x1, Pallas kernels, on_device(): pl.pallas_call(functools.partial(correlate_kernel, blk, chan, chn, spectr...  11.9 us
    pallas_call x1, Pallas kernels, on_device(): pl.pallas_call(functools.partial(spectra_kernel, frames, parts), out_shap...  7.65 us
    pallas_call x1, Pallas kernels, on_device(): pl.pallas_call(functools.partial(finish_kernel, blk, chn, feeds), out_sha...  3.31 us
    ppermute x1, starting transfers between devices, on_device(): halo = lax.ppermute(last, 'chan', [(a, a + 1) for a in range(chan - 1)])  2.39 us
  transfers between devices with their start and end apart: 1, of which 1 were waited for; matrix products, arithmetic and copies ran while one was open for 0% of the time, Pallas kernels for 0%

profile of v1, /device:TPU:0, one launch (start us, length us, event | category | flops | bytes accessed | tf_op | source)
XLA Modules:
  0.0 99.6 jit_solution(962065020794946050)
XLA Ops:
  0.0 1.0 %slice.3 = bf16[8,28672]{1,0:T(8,128)(2,1)S(1)} slice(bf16[8,65536]{1,0:T(8,128)(2,1)} %volt.1), slice={[0:8], [36864:65536]} | slice | bytes 917504 | tf_op jit(solution)/shard_map/slice | solution.py:220
  1.1 2.4 %collective-permute-start = (bf16[8,28672]{1,0:T(8,128)(2,1)S(1)}, bf16[8,28672]{1,0:T(8,128)(2,1)S(1)}, u32[]{:S(2)}, u32[]{:S(2)}) collective-permute-start(bf16[8,28672]{1,0:T(8,128)(2,1)S(1)} %slice.3), channel_id=1, source_target_pairs={{0,8},{8,16},{16,24},{1,9},{9,17},{17,25},{2,10},{10,18},{18,26},{... | collective-permute-start | bytes 1376264 | tf_op jit(solution)/shard_map/ppermute | solution.py:221
  3.4 1.4 %collective-permute-done.halo = bf16[8,28672]{1,0:T(8,128)(2,1)S(1)} collective-permute-done((bf16[8,28672]{1,0:T(8,128)(2,1)S(1)}, bf16[8,28672]{1,0:T(8,128)(2,1)S(1)}, u32[]{:S(2)}, u32[]{:S(2)}) %collective-permute-start) | collective-permute-done | bytes 458784 | tf_op jit(solution)/shard_map/ppermute | solution.py:221
  4.8 0.0 copy-start
  4.8 0.8 copy-done
  5.6 7.7 %spectra.1 = bf16[32,2,64,128]{3,2,1,0:T(8,128)(2,1)} custom-call(bf16[8,65536]{1,0:T(8,128)(2,1)} %volt.1, bf16[8,28672]{1,0:T(8,128)(2,1)} %copy-done, f32[8,4096]{1,0:T(8,128)} %taps.1, f32[2,32,128]{2,1,0:T(8,128)} %constant.6.clone.twiddle, bf16[128,256]{1,0:T(8,128)(2,1)} %constant.7.clone.high, bf16[128,256]{1,0:T(8,128)(2,1)} %constant.8.clone.low), custom_call_target="tpu_custom_call" | custom-call | tf_op jit(solution)/shard_map/spectra/pallas_call | solution.py:223
  13.3 41.0 %all_to_all.10.seen = bf16[32,2,64,128]{3,2,1,0:T(8,128)(2,1)} all-to-all(bf16[32,2,64,128]{3,2,1,0:T(8,128)(2,1)} %spectra.1), channel_id=1, replica_groups=mesh['chan'=4,'blk'=8] {'chan','blk'}, dimensions={0} | all-to-all | bytes 2097152 | tf_op jit(solution)/shard_map/all_to_all | solution.py:236
  54.3 11.9 %correlate.1 = bf16[8,512,128]{2,1,0:T(8,128)(2,1)} custom-call(bf16[32,2,64,128]{3,2,1,0:T(8,128)(2,1)} %all_to_all.10.seen), custom_call_target="tpu_custom_call" | custom-call | tf_op jit(solution)/shard_map/correlate/pallas_call | solution.py:237
  66.2 30.1 %all_to_all.11.seen = bf16[8,512,128]{2,1,0:T(8,128)(2,1)} all-to-all(bf16[8,512,128]{2,1,0:T(8,128)(2,1)} %correlate.1), channel_id=1, replica_groups=mesh['chan'=4,'blk'=8] {'blk'}, dimensions={0} | all-to-all | bytes 2097152 | tf_op jit(solution)/shard_map/all_to_all | solution.py:246
  96.3 3.3 %finish.1 = f32[2,8,64,512]{3,2,1,0:T(8,128)} custom-call(bf16[8,512,128]{2,1,0:T(8,128)(2,1)} %all_to_all.11.seen), custom_call_target="tpu_custom_call" | custom-call | tf_op jit(solution)/shard_map/finish/pallas_call | solution.py:247
Async XLA Ops:
  1.1 3.8 %collective-permute-start = (bf16[8,28672]{1,0:T(8,128)(2,1)S(1)}, bf16[8,28672]{1,0:T(8,128)(2,1)S(1)}, u32[]{:S(2)}, u32[]{:S(2)}) collective-permute-start(bf16[8,28672]{1,0:T(8,128)(2,1)S(1)} %slice.3), channel_id=1, source_target_pairs={{0,8},{8,16},{16,24},{1,9},{9,17},{17,25},{2,10},{10,18},{18,26},{... | collective-permute-start | bytes 1376264 | tf_op jit(solution)/shard_map/ppermute | solution.py:221
  4.8 0.8 copy-start

commit v2 on v1

--- a/solution.py
+++ b/solution.py
@@ -65,21 +65,29 @@
 
 
 def fir_stage(volt, halo, taps, filtered, frames):
+    first, end = frames
+
     @pl.loop(0, N1)
     def _(n1):
         lane = pl.multiple_of(n1 * N2, N2)
         weights = [jnp.broadcast_to(taps[t : t + 1, pl.ds(lane, N2)], (8, N2)) for t in range(TAPS)]
-        window = [halo[:, pl.ds(f * L + lane, N2)].astype(jnp.float32) for f in range(TAPS - 1)]
-        for f in range(frames):
-            window.append(volt[:, pl.ds(f * L + lane, N2)].astype(jnp.float32))
+
+        def frame(f):
+            if f < 0:
+                return halo[:, pl.ds((f + TAPS - 1) * L + lane, N2)].astype(jnp.float32)
+            return volt[:, pl.ds(f * L + lane, N2)].astype(jnp.float32)
+
+        window = [frame(f) for f in range(first - TAPS + 1, first)]
+        for f in range(end - first):
+            window.append(frame(first + f))
             total = weights[0] * window[f]
             for t in range(1, TAPS):
                 total = total + weights[t] * window[f + t]
-            filtered[f * N1 + n1] = total
+            filtered[(first + f) * N1 + n1] = total
 
 
 def first_stage(filtered, twiddle, turned, frames):
-    @pl.loop(0, frames)
+    @pl.loop(*frames)
     def _(f):
         spectrum = real_dft([filtered[f * N1 + n1] for n1 in range(N1)])
         row = pl.multiple_of(f * 8, 8)
@@ -101,30 +109,16 @@
             turned[k1, pl.ds(row, 8), pl.ds(N2, N2)] = im
 
 
-def second_stage(turned, high, low, ordered):
+def second_stage(turned, k1, high, low):
     contract = (((1,), (1,)), ((), ()))
     wh, wl = high[...], low[...]
-    for k1 in range(N1):
-        z = turned[k1]
-        zh = z.astype(jnp.bfloat16)
-        zl = (z - zh.astype(jnp.float32)).astype(jnp.bfloat16)
-        out = lax.dot_general(wl, zh, contract, preferred_element_type=jnp.float32)
-        out = out + lax.dot_general(wh, zl, contract, preferred_element_type=jnp.float32)
-        out = out + lax.dot_general(wh, zh, contract, preferred_element_type=jnp.float32)
-        for p in range(2):
-            ordered[pl.ds(p * C + k1, HALF, stride=N1), :] = out[p * HALF : (p + 1) * HALF]
-
-
-def spectra_kernel(frames, parts, volt, halo, taps, twiddle, high, low, out, filtered, turned, ordered):
-    fir_stage(volt, halo, taps, filtered, frames)
-    first_stage(filtered, twiddle, turned, frames)
-    second_stage(turned, high, low, ordered)
-    chn = C // parts
-
-    @pl.loop(0, parts)
-    def _(d):
-        for p in range(2):
-            out[d, p] = ordered[pl.ds(pl.multiple_of(p * C + d * chn, chn), chn), :].astype(jnp.bfloat16)
+    z = turned[k1]
+    zh = z.astype(jnp.bfloat16)
+    zl = (z - zh.astype(jnp.float32)).astype(jnp.bfloat16)
+    out = lax.dot_general(wl, zh, contract, preferred_element_type=jnp.float32)
+    out = out + lax.dot_general(wh, zl, contract, preferred_element_type=jnp.float32)
+    out = out + lax.dot_general(wh, zh, contract, preferred_element_type=jnp.float32)
+    return out.astype(jnp.bfloat16)
 
 
 def regroup(groups, lane):
@@ -176,25 +170,145 @@
             put(b, pl.multiple_of(h * 16, 16), rows.astype(jnp.bfloat16))
 
 
-def correlate_kernel(blk, chan, chn, spectra_count, seen, out, grouped):
-    gather_feeds(lambda c, b, p: seen[c * blk + b, p], blk, chan, chn, grouped)
-
-    def put(b, row, rows):
-        out[b, pl.ds(row, 16), :] = rows
-
-    correlate(grouped, blk, chan, chn, spectra_count, put)
-
-
-def finish(get, blk, chn, feeds, out, wide):
+def exchange_kernel(
+    sizes, volt, taps, twiddle, high, low, out,
+    halo, filtered, turned, sent, seen, grouped, products,
+    halo_sems, send_sems, seen_sems, product_sems, out_sem,
+):
+    frames, chan, blk = sizes
+    parts = chan * blk
+    width = HALF // chan
+    per = N1 // blk
+    chunks, held = sent.shape[0], per // sent.shape[0]
+    c, b = lax.axis_index("chan"), lax.axis_index("blk")
+    barrier = pltpu.get_barrier_semaphore()
+
+    @pl.loop(1, parts)
+    def _(d):
+        other = lax.rem(c * blk + b + d, parts)
+        pl.semaphore_signal(
+            barrier,
+            inc=1,
+            device_id={"chan": lax.div(other, blk), "blk": lax.rem(other, blk)},
+            device_id_type=pl.DeviceIdType.MESH,
+        )
+
+    @pl.when(c == 0)
+    def _():
+        halo[...] = jnp.zeros_like(halo)
+
+    late, early = (TAPS - 1, frames), (0, TAPS - 1)
+    fir_stage(volt, halo, taps, filtered, late)
+    pl.semaphore_wait(barrier, parts - 1)
+    halo_copy = pltpu.make_async_remote_copy(
+        src_ref=volt.at[:, pl.ds((frames - TAPS + 1) * L, (TAPS - 1) * L)],
+        dst_ref=halo,
+        send_sem=halo_sems.at[0],
+        recv_sem=halo_sems.at[1],
+        device_id={"chan": lax.rem(c + 1, chan), "blk": b},
+        device_id_type=pl.DeviceIdType.MESH,
+    )
+
+    @pl.when(c < chan - 1)
+    def _():
+        halo_copy.start()
+
+    first_stage(filtered, twiddle, turned, late)
+
+    @pl.when(c > 0)
+    def _():
+        halo_copy.wait_recv()
+
+    fir_stage(volt, halo, taps, filtered, early)
+    first_stage(filtered, twiddle, turned, early)
+
+    me = c * blk + b
+    for q in range(chunks):
+
+        @pl.loop(0, blk)
+        def _(t):
+            to_b = lax.rem(b + blk // 2 + t, blk)
+            for kk in range(held):
+                value = second_stage(turned, to_b * per + q * held + kk, high, low)
+                for to_c in range(chan):
+                    for p in range(2):
+                        row = p * HALF + to_c * width
+                        sent[q, to_c * blk + to_b, pl.ds((kk * 2 + p) * width, width), :] = value[row : row + width]
+            for u in range(chan):
+                to_c = lax.rem(c + u, chan)
+                to = to_c * blk + to_b
+                copy = pltpu.make_async_remote_copy(
+                    src_ref=sent.at[q, to],
+                    dst_ref=seen.at[q, me],
+                    send_sem=send_sems.at[q],
+                    recv_sem=seen_sems.at[q],
+                    device_id={"chan": to_c, "blk": to_b},
+                    device_id_type=pl.DeviceIdType.MESH,
+                )
+                if u == 0:
+                    pl.when(to_b != b)(copy.start)
+
+                    @pl.when(to_b == b)
+                    def _():
+                        pltpu.make_async_copy(sent.at[q, me], seen.at[q, me], seen_sems.at[q]).start()
+                else:
+                    copy.start()
+
+    for q in range(chunks):
+        pltpu.make_async_copy(seen.at[q], seen.at[q], seen_sems.at[q]).wait()
+        for kk in range(held):
+
+            def get(from_c, from_b, p):
+                return seen[q, from_c * blk + from_b, pl.ds((kk * 2 + p) * width, width), :]
+
+            index = q * held + kk
+
+            def put(to_b, row, rows):
+                products[index, to_b, pl.ds(row, 16), :] = rows
+
+            gather_feeds(get, blk, chan, width, grouped)
+            correlate(grouped, blk, chan, width, frames * chan, put)
+
+            @pl.loop(0, blk - 1)
+            def _(t):
+                to_b = lax.rem(b + 1 + lax.rem(t + blk // 2 - 1, blk - 1), blk)
+                pltpu.make_async_remote_copy(
+                    src_ref=products.at[index, to_b],
+                    dst_ref=out.at[index, b],
+                    send_sem=product_sems.at[index],
+                    recv_sem=out_sem,
+                    device_id={"chan": c, "blk": to_b},
+                    device_id_type=pl.DeviceIdType.MESH,
+                ).start()
+
+            pltpu.make_async_copy(products.at[index, b], out.at[index, b], out_sem).start()
+
+    pltpu.make_async_copy(out, out, out_sem).wait()
+    for q in range(chunks):
+        part = sent.at[q, pl.ds(0, parts - 1)]
+        pltpu.make_async_copy(part, part, send_sems.at[q]).wait()
+    for index in range(per):
+        part = products.at[index, pl.ds(0, blk - 1)]
+        pltpu.make_async_copy(part, part, product_sems.at[index]).wait()
+
+    @pl.when(c < chan - 1)
+    def _():
+        halo_copy.wait_send()
+
+
+def finish_kernel(blk, per, width, feeds, seen, out, wide):
     @pl.loop(0, blk)
     def _(b):
-        for first in range(0, 2 * feeds, 128):
-            value = get(b, first).astype(jnp.float32)
-            wide[first // 128, pl.ds(pl.multiple_of(b * chn * 8, chn * 8), chn * 8), :] = value
+        for kk in range(per):
+            for first in range(0, 2 * feeds, 128):
+                value = seen[kk, b, :, first : first + 128].astype(jnp.float32)
+                for k2 in range(width):
+                    row = pl.multiple_of((k2 * N1 + b * per + kk) * 8, 8)
+                    wide[first // 128, pl.ds(row, 8), :] = value[k2 * 8 : k2 * 8 + 8]
 
     piece = min(feeds, 128)
     for i in range(8):
-        for block in range(0, blk * chn, 128):
+        for block in range(0, width * N1, 128):
             for first in range(0, 2 * feeds, 128):
                 tile = wide[first // 128, pl.ds(block * 8 + i, 128, stride=8), :].T
                 for at in range(0, 128, piece):
@@ -202,10 +316,6 @@
                     out[part, i, pl.ds(j, piece), pl.ds(block, 128)] = tile[at : at + piece]
 
 
-def finish_kernel(blk, chn, feeds, seen, out, wide):
-    finish(lambda b, first: seen[b, :, first : first + 128], blk, chn, feeds, out, wide)
-
-
 def whole(count):
     return [pl.BlockSpec(memory_space=pltpu.VMEM)] * count
 
@@ -213,44 +323,41 @@
 def on_device(chan, blk, voltages, fir_taps):
     frames = voltages.shape[1] // L
     parts = chan * blk
-    chn = C // parts
     feeds = blk * 8
-    spectra_count = frames * chan
+    per, width = N1 // blk, HALF // chan
+    chunks = min(per, 2)
+    rows = 2 * width * per // chunks
     twiddle, high, low = tables()
-    last = voltages[:, (frames - TAPS + 1) * L :]
-    halo = lax.ppermute(last, "chan", [(a, a + 1) for a in range(chan - 1)])
-    params = pltpu.CompilerParams(vmem_limit_bytes=VMEM)
-    spectra = pl.pallas_call(
-        functools.partial(spectra_kernel, frames, parts),
-        out_shape=jax.ShapeDtypeStruct((parts, 2, chn, 128), jnp.bfloat16),
-        in_specs=whole(6),
-        out_specs=whole(1)[0],
+    dma = pltpu.SemaphoreType.DMA
+    mine = pl.pallas_call(
+        functools.partial(exchange_kernel, (frames, chan, blk)),
+        out_shape=jax.ShapeDtypeStruct((per, blk, width * 8, 2 * feeds), jnp.bfloat16),
+        in_specs=whole(5),
+        out_specs=pl.BlockSpec(memory_space=pl.ANY),
         scratch_shapes=[
+            pltpu.VMEM((8, (TAPS - 1) * L), jnp.bfloat16),
             pltpu.VMEM((frames * N1, 8, N2), jnp.float32),
             pltpu.VMEM((N1, 8 * frames, 2 * N2), jnp.float32),
-            pltpu.VMEM((2 * C, 8 * frames), jnp.float32),
+            pltpu.VMEM((chunks, parts, rows, 128), jnp.bfloat16),
+            pltpu.VMEM((chunks, parts, rows, 128), jnp.bfloat16),
+            pltpu.VMEM((feeds * width, 128), jnp.float32),
+            pltpu.VMEM((per, blk, width * 8, 2 * feeds), jnp.bfloat16),
+            dma((2,)),
+            dma((chunks,)),
+            dma((chunks,)),
+            dma((per,)),
+            dma,
         ],
-        compiler_params=params,
-        name="spectra",
-    )(voltages, halo, fir_taps, jnp.asarray(twiddle), jnp.asarray(high), jnp.asarray(low))
-    seen = lax.all_to_all(spectra, ("chan", "blk"), split_axis=0, concat_axis=0, tiled=True)
-    products = pl.pallas_call(
-        functools.partial(correlate_kernel, blk, chan, chn, spectra_count),
-        out_shape=jax.ShapeDtypeStruct((blk, chn * 8, 2 * feeds), jnp.bfloat16),
+        compiler_params=pltpu.CompilerParams(vmem_limit_bytes=VMEM, collective_id=0, has_side_effects=True),
+        name="exchange",
+    )(voltages, fir_taps, jnp.asarray(twiddle), jnp.asarray(high), jnp.asarray(low))
+    return pl.pallas_call(
+        functools.partial(finish_kernel, blk, per, width, feeds),
+        out_shape=jax.ShapeDtypeStruct((2, 8, feeds, width * N1), jnp.float32),
         in_specs=whole(1),
         out_specs=whole(1)[0],
-        scratch_shapes=[pltpu.VMEM((feeds * chn, 128), jnp.float32)],
-        compiler_params=params,
-        name="correlate",
-    )(seen)
-    mine = lax.all_to_all(products, "blk", split_axis=0, concat_axis=0, tiled=True)
-    return pl.pallas_call(
-        functools.partial(finish_kernel, blk, chn, feeds),
-        out_shape=jax.ShapeDtypeStruct((2, 8, feeds, blk * chn), jnp.float32),
-        in_specs=whole(1),
-        out_specs=whole(1)[0],
-        scratch_shapes=[pltpu.VMEM((feeds // 64, blk * chn * 8, 128), jnp.float32)],
-        compiler_params=params,
+        scratch_shapes=[pltpu.VMEM((feeds // 64, width * N1 * 8, 128), jnp.float32)],
+        compiler_params=pltpu.CompilerParams(vmem_limit_bytes=VMEM),
         name="finish",
     )(mine)
 

time: 100 us -> 63.3 us (0.63)
  blocking collectives: 71.1 us -> 0 us
  Pallas kernels: 22.9 us -> 63.1 us
  starting transfers between devices: 2.39 us -> 0 us
  local copies, waits for them, and re-layouts: 1.81 us -> 0 us
  waiting for transfers between devices: 1.4 us -> 0 us
    all_to_all x2 -> x0, blocking collectives: 71.1 us -> none  [the longest x1 41 us: on_device(): lax.all_to_all(spectra, ('chan', 'blk'), split_axis=0, concat_axis=0, til...]
    pallas_call x3 -> x2, Pallas kernels: 22.9 us -> 63.1 us  [the longest x1 59.8 us: on_device(): pl.pallas_call(functools.partial(exchange_kernel, (frames, chan, blk)), o...]
    ppermute x1 -> x0, starting transfers between devices: 2.39 us -> none  [on_device(): halo = lax.ppermute(last, 'chan', [(a, a + 1) for a in range(chan - 1)])]
    ppermute x1 -> x0, waiting for transfers between devices: 1.4 us -> none  [on_device(): halo = lax.ppermute(last, 'chan', [(a, a + 1) for a in range(chan - 1)])]
    slice x1 -> x0, local copies, waits for them, and re-layouts: 1.05 us -> none  [on_device(): last = voltages[:, (frames - TAPS + 1) * L:]]
  transfers between devices with their start and end apart: 1 -> 0, of which waited for: 1 -> 0; matrix products, arithmetic and copies ran while one was open for 0% -> 0% of each run, Pallas kernels for 0% -> 0%
where the time goes in v2:
time: 63.3 us; the launch traced here: 63.1 us
  Pallas kernels  63.1 us (100%)
    pallas_call x1, Pallas kernels, on_device(): pl.pallas_call(functools.partial(exchange_kernel, (frames, chan, blk)), o...  59.8 us
    pallas_call x1, Pallas kernels, on_device(): pl.pallas_call(functools.partial(finish_kernel, blk, per, width, feeds),...  3.37 us

profile of v2, /device:TPU:0, one launch (start us, length us, event | category | flops | bytes accessed | tf_op | source)
XLA Modules:
  0.0 63.1 jit_solution(9061415427086844622)
XLA Ops:
  0.0 59.8 %exchange.1.seen = bf16[4,8,128,128]{3,2,1,0:T(8,128)(2,1)} custom-call(bf16[8,65536]{1,0:T(8,128)(2,1)} %volt.1, f32[8,4096]{1,0:T(8,128)} %taps.1, f32[2,32,128]{2,1,0:T(8,128)} %constant.6.clone.twiddle, bf16[128,256]{1,0:T(8,128)(2,1)} %constant.7.clone.high, bf16[128,256]{1,0:T(8,128)(2,1)} %constant.8.clone.low), custom_call_target="tpu_custom_call" | custom-call | tf_op jit(solution)/shard_map/exchange/pallas_call | solution.py:332
  59.8 3.4 %finish.1 = f32[2,8,64,512]{3,2,1,0:T(8,128)} custom-call(bf16[4,8,128,128]{3,2,1,0:T(8,128)(2,1)} %exchange.1.seen), custom_call_target="tpu_custom_call" | custom-call | tf_op jit(solution)/shard_map/finish/pallas_call | solution.py:354

commit v3 on v2

v3 whole, which is shorter than its diff:
```python
import functools
import math

import jax
import jax.numpy as jnp
import numpy as np
from jax import lax
from jax.experimental import pallas as pl
from jax.experimental.pallas import tpu as pltpu
from jax.sharding import PartitionSpec as P

TAPS = 8
L = 4096
C = 2048
N2 = 128
N1 = L // N2
HALF = C // N1
VMEM = 56 * 1024 * 1024


def tables():
    n2 = np.arange(N2)
    angle = 2.0 * np.pi * (np.arange(N1)[:, None] * n2[None, :] % L) / L
    twiddle = np.stack([np.cos(angle), np.sin(angle)]).astype(np.float32)
    angle = 2.0 * np.pi * (np.arange(HALF)[:, None] * n2[None, :] % N2) / N2
    cos, sin = np.cos(angle) / math.sqrt(L), np.sin(angle) / math.sqrt(L)
    matrix = np.block([[cos, sin], [-sin, cos]])
    high = matrix.astype(jnp.bfloat16)
    low = (matrix - high.astype(np.float64)).astype(jnp.bfloat16)
    return twiddle, high, low


def times(scale, value):
    return None if value is None else scale * value


def plus(a, b):
    return b if a is None else a if b is None else a + b


def minus(a, b):
    return a if b is None else -b if a is None else a - b


def real_dft(values):
    n = len(values)
    if n == 1:
        return [(values[0], None)]
    half = n // 2
    even, odd = real_dft(values[0::2]), real_dft(values[1::2])
    result = [None] * (half + 1)
    for k in range(half // 2 + 1):
        (er, ei), (odr, odi) = even[k], odd[k]
        if k == 0:
            tr, ti = odr, odi
        elif 4 * k == n:
            tr, ti = odi, -odr
        else:
            c, s = math.cos(2 * math.pi * k / n), math.sin(2 * math.pi * k / n)
            tr = plus(times(c, odr), times(s, odi))
            ti = minus(times(c, odi), times(s, odr))
        result[half - k] = (minus(er, tr), minus(ti, ei))
        result[k] = (plus(er, tr), plus(ei, ti))
    return result


def fir_stage(volt, halo, taps, filtered, frames):
    first, end = frames

    @pl.loop(0, N1)
    def _(n1):
        lane = pl.multiple_of(n1 * N2, N2)
        weights = [jnp.broadcast_to(taps[t : t + 1, pl.ds(lane, N2)], (8, N2)) for t in range(TAPS)]

        def frame(f):
            if f < 0:
                return halo[:, pl.ds((f + TAPS - 1) * L + lane, N2)].astype(jnp.float32)
            return volt[:, pl.ds(f * L + lane, N2)].astype(jnp.float32)

        window = [frame(f) for f in range(first - TAPS + 1, first)]
        for f in range(end - first):
            window.append(frame(first + f))
            total = weights[0] * window[f]
            for t in range(1, TAPS):
                total = total + weights[t] * window[f + t]
            filtered[(first + f) * N1 + n1] = total


def first_stage(filtered, twiddle, turned, frames):
    @pl.loop(*frames)
    def _(f):
        spectrum = real_dft([filtered[f * N1 + n1] for n1 in range(N1)])
        row = pl.multiple_of(f * 8, 8)
        for k1 in range(N1):
            if 2 * k1 <= N1:
                zr, zi = spectrum[k1]
            else:
                zr, zi = spectrum[N1 - k1]
                zi = -zi
            c = twiddle[0, k1 : k1 + 1, :]
            s = twiddle[1, k1 : k1 + 1, :]
            if k1 == 0:
                re, im = zr, jnp.zeros_like(zr)
            elif zi is None:
                re, im = c * zr, -(s * zr)
            else:
                re, im = c * zr + s * zi, c * zi - s * zr
            turned[k1, pl.ds(row, 8), pl.ds(0, N2)] = re
            turned[k1, pl.ds(row, 8), pl.ds(N2, N2)] = im


def second_stage(turned, k1, high, low):
    contract = (((1,), (1,)), ((), ()))
    wh, wl = high[...], low[...]
    z = turned[k1]
    zh = z.astype(jnp.bfloat16)
    zl = (z - zh.astype(jnp.float32)).astype(jnp.bfloat16)
    out = lax.dot_general(wl, zh, contract, preferred_element_type=jnp.float32)
    out = out + lax.dot_general(wh, zl, contract, preferred_element_type=jnp.float32)
    out = out + lax.dot_general(wh, zh, contract, preferred_element_type=jnp.float32)
    return out.astype(jnp.bfloat16)


def regroup(groups, lane):
    count = len(groups)
    d = 1
    while d < count:
        low_side = (lane & d) == 0
        result = list(groups)
        for g in range(count):
            if g & d == 0:
                a, b = groups[g], groups[g | d]
                result[g] = jnp.where(low_side, a, pltpu.roll(b, d, 1))
                result[g | d] = jnp.where(low_side, pltpu.roll(a, 128 - d, 1), b)
        groups = result
        d *= 2
    return groups


def gather_feeds(get, blk, chan, width, place, grouped):
    lane = lax.broadcasted_iota(jnp.int32, (width, 128), 1)

    @pl.loop(0, blk)
    def _(b):
        arrays = [get(c, b, p).astype(jnp.float32) for p in range(2) for c in range(chan)]
        for feed, value in enumerate(regroup(arrays, lane)):
            row = pl.multiple_of((place(b) * 8 + feed) * width, width)
            grouped[pl.ds(row, width), :] = value


def sides(grouped, ch, feeds, width, chan):
    lane = lax.broadcasted_iota(jnp.int32, (feeds, 128), 1)
    value = grouped[pl.ds(ch, feeds, stride=width), :]
    other = jnp.where((lane & chan) == 0, -pltpu.roll(value, 128 - chan, 1), pltpu.roll(value, chan, 1))
    return value.astype(jnp.bfloat16), other.astype(jnp.bfloat16)


def product(left, right):
    return lax.dot_general(left, right, (((1,), (1,)), ((), ())), preferred_element_type=jnp.float32)


def paired(lefts, rights):
    zero = jnp.zeros_like(rights[0])
    right = jnp.concatenate(
        [jnp.concatenate([rights[0], zero], axis=1), jnp.concatenate([zero, rights[1]], axis=1)], axis=0
    )
    return product(jnp.concatenate(lefts, axis=1), right)


def correlate(grouped, nearby, half, chan, width, spectra_count, near, far):
    near_feeds = half * 8
    feeds = 2 * near_feeds
    scale = 1.0 / spectra_count

    @pl.loop(0, width // 4)
    def _(quad):
        far_rows, own_rows, full_rows = [], [], []
        for pair in range(2):
            lefts, rights, own_lefts, own_rights, full = [], [], [], [], []
            for one in range(2):
                ch = quad * 4 + pair * 2 + one
                value, other = sides(grouped, ch, feeds, width, chan)
                right = jnp.concatenate([value[:near_feeds], other[:near_feeds]], axis=0)
                rest = jnp.concatenate([value[near_feeds:], other[near_feeds:]], axis=0)
                full.append(product(value[:near_feeds], jnp.concatenate([right, rest], axis=0)) * scale)
                lefts.append(value[near_feeds:])
                rights.append(right)
                value, other = sides(nearby, ch, near_feeds, width, chan)
                own_lefts.append(value)
                own_rights.append(jnp.concatenate([value, other], axis=0))
            full_rows.append(full)
            far_rows.append(paired(lefts, rights) * scale)
            own_rows.append(paired(own_lefts, own_rights) * scale)
        for b in range(half):
            cut = slice(b * 8, b * 8 + 8)

            def put(ref, row, first, second):
                rows = jnp.concatenate([first[cut], second[cut]], axis=0)
                ref[b, pl.ds(pl.multiple_of(row, 16), 16), :] = rows.astype(jnp.bfloat16)

            for pair in range(2):
                put(near, (quad * 2 + pair) * 16, *full_rows[pair])
            put(near, width * 8 + quad * 16, *own_rows)
            put(far, quad * 16, *far_rows)


def exchange_kernel(
    sizes, volt, taps, twiddle, high, low, out_near, out_far,
    halo, filtered, turned, sent, seen, seen_near, grouped, nearby, near, far,
    halo_sems, send_sems, seen_sems, product_sems, out_sems,
):
    frames, chan, blk = sizes
    parts, half = chan * blk, blk // 2
    width = HALF // chan
    per = N1 // blk
    chunks, held = sent.shape[0], per // sent.shape[0]
    c, b = lax.axis_index("chan"), lax.axis_index("blk")
    side, spot = lax.div(b, half), lax.rem(b, half)
    barrier = pltpu.get_barrier_semaphore()

    def remote(src, dst, send_sem, recv_sem, to_c, to_b):
        return pltpu.make_async_remote_copy(
            src_ref=src,
            dst_ref=dst,
            send_sem=send_sem,
            recv_sem=recv_sem,
            device_id={"chan": to_c, "blk": to_b},
            device_id_type=pl.DeviceIdType.MESH,
        )

    @pl.loop(1, parts)
    def _(d):
        other = lax.rem(c * blk + b + d, parts)
        pl.semaphore_signal(
            barrier,
            inc=1,
            device_id={"chan": lax.div(other, blk), "blk": lax.rem(other, blk)},
            device_id_type=pl.DeviceIdType.MESH,
        )

    @pl.when(c == 0)
    def _():
        halo[...] = jnp.zeros_like(halo)

    late, early = (TAPS - 1, frames), (0, TAPS - 1)
    fir_stage(volt, halo, taps, filtered, late)
    pl.semaphore_wait(barrier, parts - 1)
    last = volt.at[:, pl.ds((frames - TAPS + 1) * L, (TAPS - 1) * L)]
    halo_copy = remote(last, halo, halo_sems.at[0], halo_sems.at[1], lax.rem(c + 1, chan), b)

    @pl.when(c < chan - 1)
    def _():
        halo_copy.start()

    first_stage(filtered, twiddle, turned, late)

    @pl.when(c > 0)
    def _():
        halo_copy.wait_recv()

    fir_stage(volt, halo, taps, filtered, early)
    first_stage(filtered, twiddle, turned, early)

    for q in range(chunks):

        @pl.loop(0, half)
        def _(t):
            at = lax.rem(spot + 1 + t, half)
            near_b, far_b = side * half + at, (1 - side) * half + at
            for to_b in (far_b, near_b):
                for kk in range(held):
                    value = second_stage(turned, to_b * per + q * held + kk, high, low)
                    for to_c in range(chan):
                        for p in range(2):
                            row = p * HALF + to_c * width
                            place = pl.ds((kk * 2 + p) * width, width)
                            sent[q, to_c * blk + to_b, place, :] = value[row : row + width]
                if to_b is far_b:
                    for u in range(chan):
                        to_c = lax.rem(c + u, chan)
                        block = sent.at[q, to_c * blk + far_b]
                        remote(
                            block, seen.at[q, c * blk + b], send_sems.at[0, q], seen_sems.at[0, q], to_c, far_b
                        ).start()
            for u in range(chan):
                to_c = lax.rem(c + u, chan)
                for kind, to_b, dst in (
                    (0, near_b, seen.at[q, c * blk + b]),
                    (1, far_b, seen_near.at[q, c * half + spot]),
                ):
                    block = sent.at[q, to_c * blk + to_b]
                    copy = remote(block, dst, send_sems.at[kind, q], seen_sems.at[kind, q], to_c, near_b)
                    if u == 0:
                        pl.when(near_b != b)(copy.start)
                        pl.when(near_b == b)(pltpu.make_async_copy(block, dst, seen_sems.at[kind, q]).start)
                    else:
                        copy.start()

    for q in range(chunks):
        for kind, ref in enumerate((seen, seen_near)):
            pltpu.make_async_copy(ref.at[q], ref.at[q], seen_sems.at[kind, q]).wait()
        for kk in range(held):

            def get(from_c, from_b, p):
                return seen[q, from_c * blk + from_b, pl.ds((kk * 2 + p) * width, width), :]

            def get_near(from_c, at, p):
                return seen_near[q, from_c * half + at, pl.ds((kk * 2 + p) * width, width), :]

            index = q * held + kk
            gather_feeds(get, blk, chan, width, lambda from_b: lax.rem(from_b + side * half, blk), grouped)
            gather_feeds(get_near, half, chan, width, lambda at: at, nearby)
            correlate(grouped, nearby, half, chan, width, frames * chan, near.at[index], far.at[index])

            @pl.loop(0, half)
            def _(t):
                at = lax.rem(spot + 1 + t, half)
                near_b, far_b = side * half + at, (1 - side) * half + at
                remote(
                    far.at[index, at], out_far.at[index, spot], product_sems.at[1, index], out_sems.at[1], c, far_b
                ).start()
                copy = remote(
                    near.at[index, at], out_near.at[index, spot], product_sems.at[0, index], out_sems.at[0], c, near_b
                )
                pl.when(at != spot)(copy.start)

            pltpu.make_async_copy(near.at[index, spot], out_near.at[index, spot], out_sems.at[0]).start()

    pltpu.make_async_copy(out_near, out_near, out_sems.at[0]).wait()
    pltpu.make_async_copy(out_far, out_far, out_sems.at[1]).wait()
    for q in range(chunks):
        for kind, count in enumerate((parts, chan * half)):
            part = sent.at[q, pl.ds(0, count - 1)]
            pltpu.make_async_copy(part, part, send_sems.at[kind, q]).wait()
    for index in range(per):
        part = near.at[index, pl.ds(0, half - 1)]
        pltpu.make_async_copy(part, part, product_sems.at[0, index]).wait()
        pltpu.make_async_copy(far.at[index], far.at[index], product_sems.at[1, index]).wait()

    @pl.when(c < chan - 1)
    def _():
        halo_copy.wait_send()


def join(first, second, feeds):
    if feeds % 128 == 0:
        return [
            jnp.concatenate([first[:, cut], second[:, cut]], axis=1)
            for cut in (slice(0, feeds), slice(feeds, 2 * feeds))
        ]
    lane = lax.broadcasted_iota(jnp.int32, first.shape, 1)
    low_side = lane < feeds
    return [
        jnp.where(low_side, first, pltpu.roll(second, feeds, 1)),
        jnp.where(low_side, pltpu.roll(first, feeds, 1), second),
    ]


def finish_kernel(blk, per, width, feeds, near, far, out, wide):
    half = blk // 2
    side = lax.div(lax.axis_index("blk"), half)

    def put(k2, k1, rows):
        row = pl.multiple_of((k2 * N1 + k1) * 8, 8)
        for first in range(0, 2 * feeds, 128):
            wide[first // 128, pl.ds(row, 8), :] = rows[:, first : first + 128]

    @pl.loop(0, half)
    def _(at):
        near_b, far_b = side * half + at, (1 - side) * half + at
        for kk in range(per):
            value = near[kk, at].astype(jnp.float32)
            other = far[kk, at].astype(jnp.float32)
            for k2 in range(width):
                put(k2, near_b * per + kk, value[k2 * 8 : k2 * 8 + 8])
            for pair in range(width // 2):
                own = value[(width + pair) * 8 : (width + pair) * 8 + 8]
                for one, rows in enumerate(join(own, other[pair * 8 : pair * 8 + 8], feeds)):
                    put(2 * pair + one, far_b * per + kk, rows)

    count = feeds // 2
    piece = min(count, 128)
    for i in range(8):
        for block in range(0, width * N1, 128):
            for first in range(0, 2 * feeds, 128):
                tile = wide[first // 128, pl.ds(block * 8 + i, 128, stride=8), :].T
                for at in range(0, 128, piece):
                    which, rest = divmod(first + at, feeds)
                    part, j = divmod(rest, count)
                    start = (side if which == 0 else 1 - side) * count + j
                    out[part, i, pl.ds(pl.multiple_of(start, piece), piece), pl.ds(block, 128)] = tile[at : at + piece]


def whole(count):
    return [pl.BlockSpec(memory_space=pltpu.VMEM)] * count


def on_device(chan, blk, voltages, fir_taps):
    frames = voltages.shape[1] // L
    parts, half = chan * blk, blk // 2
    feeds = blk * 8
    per, width = N1 // blk, HALF // chan
    chunks = min(per, 2)
    rows = 2 * width * per // chunks
    twiddle, high, low = tables()
    dma = pltpu.SemaphoreType.DMA
    any_place = pl.BlockSpec(memory_space=pl.ANY)
    near = (per, half, width * 12, 2 * feeds)
    far = (per, half, width * 4, 2 * feeds)
    mine = pl.pallas_call(
        functools.partial(exchange_kernel, (frames, chan, blk)),
        out_shape=[jax.ShapeDtypeStruct(near, jnp.bfloat16), jax.ShapeDtypeStruct(far, jnp.bfloat16)],
        in_specs=whole(5),
        out_specs=[any_place, any_place],
        scratch_shapes=[
            pltpu.VMEM((8, (TAPS - 1) * L), jnp.bfloat16),
            pltpu.VMEM((frames * N1, 8, N2), jnp.float32),
            pltpu.VMEM((N1, 8 * frames, 2 * N2), jnp.float32),
            pltpu.VMEM((chunks, parts, rows, 128), jnp.bfloat16),
            pltpu.VMEM((chunks, parts, rows, 128), jnp.bfloat16),
            pltpu.VMEM((chunks, parts // 2, rows, 128), jnp.bfloat16),
            pltpu.VMEM((feeds * width, 128), jnp.float32),
            pltpu.VMEM((feeds // 2 * width, 128), jnp.float32),
            pltpu.VMEM(near, jnp.bfloat16),
            pltpu.VMEM(far, jnp.bfloat16),
            dma((2,)),
            dma((2, chunks)),
            dma((2, chunks)),
            dma((2, per)),
            dma((2,)),
        ],
        compiler_params=pltpu.CompilerParams(vmem_limit_bytes=VMEM, collective_id=0, has_side_effects=True),
        name="exchange",
    )(voltages, fir_taps, jnp.asarray(twiddle), jnp.asarray(high), jnp.asarray(low))
    return pl.pallas_call(
        functools.partial(finish_kernel, blk, per, width, feeds),
        out_shape=jax.ShapeDtypeStruct((2, 8, feeds, width * N1), jnp.float32),
        in_specs=whole(2),
        out_specs=whole(1)[0],
        scratch_shapes=[pltpu.VMEM((feeds // 64, width * N1 * 8, 128), jnp.float32)],
        compiler_params=pltpu.CompilerParams(vmem_limit_bytes=VMEM),
        name="finish",
    )(*mine)


def solution(mesh):
    chan, blk = mesh.shape["chan"], mesh.shape["blk"]
    return jax.shard_map(
        functools.partial(on_device, chan, blk),
        mesh=mesh,
        in_specs=(P("blk", "chan"), P()),
        out_specs=P(None, "blk", None, "chan"),
        check_vma=False,
    )
```

time: 63.3 us -> 56.5 us (0.89)
  Pallas kernels: 63.1 us -> 56.3 us
    pallas_call x1, Pallas kernels: 59.8 us -> 52.6 us  [on_device(): pl.pallas_call(functools.partial(exchange_kernel, (frames, chan, blk)), o...]
where the time goes in v3:
time: 56.5 us; the launch traced here: 56.3 us
  Pallas kernels  56.3 us (100%)
    pallas_call x1, Pallas kernels, on_device(): pl.pallas_call(functools.partial(exchange_kernel, (frames, chan, blk)), o...  52.6 us
    pallas_call x1, Pallas kernels, on_device(): pl.pallas_call(functools.partial(finish_kernel, blk, per, width, feeds),...  3.67 us

profile of v3, /device:TPU:0, one launch (start us, length us, event | category | flops | bytes accessed | tf_op | source)
XLA Modules:
  0.0 56.3 jit_solution(11756089198740730792)
XLA Ops:
  0.0 52.6 %exchange.1 = (bf16[4,4,192,128]{3,2,1,0:T(8,128)(2,1)}, bf16[4,4,64,128]{3,2,1,0:T(8,128)(2,1)}) custom-call(bf16[8,65536]{1,0:T(8,128)(2,1)} %volt.1, f32[8,4096]{1,0:T(8,128)} %taps.1, f32[2,32,128]{2,1,0:T(8,128)} %constant.6.clone.twiddle, bf16[128,256]{1,0:T(8,128)(2,1)} %constant.7.clone.high, bf16[128,256]{1,0:T(8,128)(2,1)} %constant.8.clone.low), custom_call_target="tpu_custom_call" | custom-call | tf_op jit(solution)/shard_map/exchange/pallas_call | solution.py:410
  52.6 3.7 %finish.1 = f32[2,8,64,512]{3,2,1,0:T(8,128)} custom-call(bf16[4,4,192,128]{3,2,1,0:T(8,128)(2,1)} %get-tuple-element.7.near, bf16[4,4,64,128]{3,2,1,0:T(8,128)(2,1)} %get-tuple-element.8.far), custom_call_target="tpu_custom_call" | custom-call | tf_op jit(solution)/shard_map/finish/pallas_call | solution.py:435

commit v4 on v3

--- a/solution.py
+++ b/solution.py
@@ -27,7 +27,7 @@
     matrix = np.block([[cos, sin], [-sin, cos]])
     high = matrix.astype(jnp.bfloat16)
     low = (matrix - high.astype(np.float64)).astype(jnp.bfloat16)
-    return twiddle, high, low
+    return twiddle, np.concatenate([low, high])
 
 
 def times(scale, value):
@@ -86,11 +86,11 @@
             filtered[(first + f) * N1 + n1] = total
 
 
-def first_stage(filtered, twiddle, turned, frames):
-    @pl.loop(*frames)
+def first_stage(filtered, twiddle, turned, part, frames):
+    @pl.loop(0, frames)
     def _(f):
-        spectrum = real_dft([filtered[f * N1 + n1] for n1 in range(N1)])
-        row = pl.multiple_of(f * 8, 8)
+        spectrum = real_dft([filtered[(part * frames + f) * N1 + n1] for n1 in range(N1)])
+        rows = pl.ds(pl.multiple_of(f * 8, 8), 8)
         for k1 in range(N1):
             if 2 * k1 <= N1:
                 zr, zi = spectrum[k1]
@@ -105,20 +105,19 @@
                 re, im = c * zr, -(s * zr)
             else:
                 re, im = c * zr + s * zi, c * zi - s * zr
-            turned[k1, pl.ds(row, 8), pl.ds(0, N2)] = re
-            turned[k1, pl.ds(row, 8), pl.ds(N2, N2)] = im
-
-
-def second_stage(turned, k1, high, low):
+            turned[part * N1 + k1, rows, pl.ds(0, N2)] = re
+            turned[part * N1 + k1, rows, pl.ds(N2, N2)] = im
+
+
+def second_stage(turned, first, second, table):
     contract = (((1,), (1,)), ((), ()))
-    wh, wl = high[...], low[...]
-    z = turned[k1]
+    z = jnp.concatenate([turned[first], turned[second]], axis=0)
     zh = z.astype(jnp.bfloat16)
     zl = (z - zh.astype(jnp.float32)).astype(jnp.bfloat16)
-    out = lax.dot_general(wl, zh, contract, preferred_element_type=jnp.float32)
-    out = out + lax.dot_general(wh, zl, contract, preferred_element_type=jnp.float32)
-    out = out + lax.dot_general(wh, zh, contract, preferred_element_type=jnp.float32)
-    return out.astype(jnp.bfloat16)
+    both = lax.dot_general(table[...], zh, contract, preferred_element_type=jnp.float32)
+    rest = lax.dot_general(table[2 * HALF :], zl, contract, preferred_element_type=jnp.float32)
+    out = both[2 * HALF :] + (both[: 2 * HALF] + rest)
+    return [value.astype(jnp.bfloat16) for value in join(out[:HALF], out[HALF:], 64)]
 
 
 def regroup(groups, lane):
@@ -142,16 +141,17 @@
 
     @pl.loop(0, blk)
     def _(b):
-        arrays = [get(c, b, p).astype(jnp.float32) for p in range(2) for c in range(chan)]
+        arrays = [get(c, b, part).astype(jnp.float32) for part in range(2) for c in range(chan)]
         for feed, value in enumerate(regroup(arrays, lane)):
             row = pl.multiple_of((place(b) * 8 + feed) * width, width)
             grouped[pl.ds(row, width), :] = value
 
 
-def sides(grouped, ch, feeds, width, chan):
+def sides(grouped, ch, feeds, width):
     lane = lax.broadcasted_iota(jnp.int32, (feeds, 128), 1)
     value = grouped[pl.ds(ch, feeds, stride=width), :]
-    other = jnp.where((lane & chan) == 0, -pltpu.roll(value, 128 - chan, 1), pltpu.roll(value, chan, 1))
+    other = pltpu.roll(value, 64, 1)
+    other = jnp.where(lane < 64, -other, other)
     return value.astype(jnp.bfloat16), other.astype(jnp.bfloat16)
 
 
@@ -167,7 +167,7 @@
     return product(jnp.concatenate(lefts, axis=1), right)
 
 
-def correlate(grouped, nearby, half, chan, width, spectra_count, near, far):
+def correlate(grouped, nearby, half, width, spectra_count, near, far):
     near_feeds = half * 8
     feeds = 2 * near_feeds
     scale = 1.0 / spectra_count
@@ -179,13 +179,13 @@
             lefts, rights, own_lefts, own_rights, full = [], [], [], [], []
             for one in range(2):
                 ch = quad * 4 + pair * 2 + one
-                value, other = sides(grouped, ch, feeds, width, chan)
+                value, other = sides(grouped, ch, feeds, width)
                 right = jnp.concatenate([value[:near_feeds], other[:near_feeds]], axis=0)
                 rest = jnp.concatenate([value[near_feeds:], other[near_feeds:]], axis=0)
                 full.append(product(value[:near_feeds], jnp.concatenate([right, rest], axis=0)) * scale)
                 lefts.append(value[near_feeds:])
                 rights.append(right)
-                value, other = sides(nearby, ch, near_feeds, width, chan)
+                value, other = sides(nearby, ch, near_feeds, width)
                 own_lefts.append(value)
                 own_rights.append(jnp.concatenate([value, other], axis=0))
             full_rows.append(full)
@@ -205,8 +205,8 @@
 
 
 def exchange_kernel(
-    sizes, volt, taps, twiddle, high, low, out_near, out_far,
-    halo, filtered, turned, sent, seen, seen_near, grouped, nearby, near, far,
+    sizes, volt, taps, twiddle, table, out_near, out_far,
+    halo, filtered, turned, sent_late, sent, seen_late, seen, near_late, seen_near, grouped, nearby, near, far,
     halo_sems, send_sems, seen_sems, product_sems, out_sems,
 ):
     frames, chan, blk = sizes
@@ -242,46 +242,26 @@
     def _():
         halo[...] = jnp.zeros_like(halo)
 
-    late, early = (TAPS - 1, frames), (0, TAPS - 1)
-    fir_stage(volt, halo, taps, filtered, late)
-    pl.semaphore_wait(barrier, parts - 1)
-    last = volt.at[:, pl.ds((frames - TAPS + 1) * L, (TAPS - 1) * L)]
-    halo_copy = remote(last, halo, halo_sems.at[0], halo_sems.at[1], lax.rem(c + 1, chan), b)
-
-    @pl.when(c < chan - 1)
-    def _():
-        halo_copy.start()
-
-    first_stage(filtered, twiddle, turned, late)
-
-    @pl.when(c > 0)
-    def _():
-        halo_copy.wait_recv()
-
-    fir_stage(volt, halo, taps, filtered, early)
-    first_stage(filtered, twiddle, turned, early)
-
-    for q in range(chunks):
-
+    def send(part, q, slot, held, sent, seen, seen_near):
         @pl.loop(0, half)
         def _(t):
             at = lax.rem(spot + 1 + t, half)
             near_b, far_b = side * half + at, (1 - side) * half + at
             for to_b in (far_b, near_b):
-                for kk in range(held):
-                    value = second_stage(turned, to_b * per + q * held + kk, high, low)
-                    for to_c in range(chan):
-                        for p in range(2):
-                            row = p * HALF + to_c * width
-                            place = pl.ds((kk * 2 + p) * width, width)
-                            sent[q, to_c * blk + to_b, place, :] = value[row : row + width]
+                base = part * N1 + to_b * per + q * held
+                for first in range(0, held, 2):
+                    second = min(first + 1, held - 1)
+                    values = second_stage(turned, base + first, base + second, table)
+                    for kk in range(first, second + 1):
+                        for to_c in range(chan):
+                            rows = pl.ds(kk * width, width)
+                            sent[q, to_c * blk + to_b, rows, :] = values[kk - first][to_c * width : (to_c + 1) * width]
                 if to_b is far_b:
                     for u in range(chan):
                         to_c = lax.rem(c + u, chan)
                         block = sent.at[q, to_c * blk + far_b]
-                        remote(
-                            block, seen.at[q, c * blk + b], send_sems.at[0, q], seen_sems.at[0, q], to_c, far_b
-                        ).start()
+                        dst = seen.at[q, c * blk + b]
+                        remote(block, dst, send_sems.at[0, slot], seen_sems.at[0, slot], to_c, far_b).start()
             for u in range(chan):
                 to_c = lax.rem(c + u, chan)
                 for kind, to_b, dst in (
@@ -289,28 +269,60 @@
                     (1, far_b, seen_near.at[q, c * half + spot]),
                 ):
                     block = sent.at[q, to_c * blk + to_b]
-                    copy = remote(block, dst, send_sems.at[kind, q], seen_sems.at[kind, q], to_c, near_b)
+                    copy = remote(block, dst, send_sems.at[kind, slot], seen_sems.at[kind, slot], to_c, near_b)
                     if u == 0:
                         pl.when(near_b != b)(copy.start)
-                        pl.when(near_b == b)(pltpu.make_async_copy(block, dst, seen_sems.at[kind, q]).start)
+                        pl.when(near_b == b)(pltpu.make_async_copy(block, dst, seen_sems.at[kind, slot]).start)
                     else:
                         copy.start()
 
+    count = frames // 2
+    fir_stage(volt, halo, taps, filtered, (count, frames))
+    pl.semaphore_wait(barrier, parts - 1)
+    last = volt.at[:, pl.ds((frames - TAPS + 1) * L, (TAPS - 1) * L)]
+    halo_copy = remote(last, halo, halo_sems.at[0], halo_sems.at[1], lax.rem(c + 1, chan), b)
+
+    @pl.when(c < chan - 1)
+    def _():
+        halo_copy.start()
+
+    first_stage(filtered, twiddle, turned, 1, count)
+    send(1, 0, 0, per, sent_late, seen_late, near_late)
+
+    @pl.when(c > 0)
+    def _():
+        halo_copy.wait_recv()
+
+    fir_stage(volt, halo, taps, filtered, (0, count))
+    first_stage(filtered, twiddle, turned, 0, count)
     for q in range(chunks):
-        for kind, ref in enumerate((seen, seen_near)):
-            pltpu.make_async_copy(ref.at[q], ref.at[q], seen_sems.at[kind, q]).wait()
+        send(0, q, 1 + q, held, sent, seen, seen_near)
+
+    def arrived(ref, kind, q, slot):
+        pltpu.make_async_copy(ref.at[q], ref.at[q], seen_sems.at[kind, slot]).wait()
+
+    arrived(seen_late, 0, 0, 0)
+    arrived(near_late, 1, 0, 0)
+    for q in range(chunks):
+        arrived(seen, 0, q, 1 + q)
+        arrived(seen_near, 1, q, 1 + q)
         for kk in range(held):
-
-            def get(from_c, from_b, p):
-                return seen[q, from_c * blk + from_b, pl.ds((kk * 2 + p) * width, width), :]
-
-            def get_near(from_c, at, p):
-                return seen_near[q, from_c * half + at, pl.ds((kk * 2 + p) * width, width), :]
-
             index = q * held + kk
+
+            def block(late, early, source, part):
+                if part == 1:
+                    return late[0, source, pl.ds(index * width, width), :]
+                return early[q, source, pl.ds(kk * width, width), :]
+
+            def get(from_c, from_b, part):
+                return block(seen_late, seen, from_c * blk + from_b, part)
+
+            def get_near(from_c, at, part):
+                return block(near_late, seen_near, from_c * half + at, part)
+
             gather_feeds(get, blk, chan, width, lambda from_b: lax.rem(from_b + side * half, blk), grouped)
             gather_feeds(get_near, half, chan, width, lambda at: at, nearby)
-            correlate(grouped, nearby, half, chan, width, frames * chan, near.at[index], far.at[index])
+            correlate(grouped, nearby, half, width, frames * chan, near.at[index], far.at[index])
 
             @pl.loop(0, half)
             def _(t):
@@ -328,13 +340,14 @@
 
     pltpu.make_async_copy(out_near, out_near, out_sems.at[0]).wait()
     pltpu.make_async_copy(out_far, out_far, out_sems.at[1]).wait()
-    for q in range(chunks):
-        for kind, count in enumerate((parts, chan * half)):
-            part = sent.at[q, pl.ds(0, count - 1)]
-            pltpu.make_async_copy(part, part, send_sems.at[kind, q]).wait()
+    for slot in range(1 + chunks):
+        ref, q = (sent_late, 0) if slot == 0 else (sent, slot - 1)
+        for kind, number in enumerate((parts, chan * half)):
+            piece = ref.at[q, pl.ds(0, number - 1)]
+            pltpu.make_async_copy(piece, piece, send_sems.at[kind, slot]).wait()
     for index in range(per):
-        part = near.at[index, pl.ds(0, half - 1)]
-        pltpu.make_async_copy(part, part, product_sems.at[0, index]).wait()
+        piece = near.at[index, pl.ds(0, half - 1)]
+        pltpu.make_async_copy(piece, piece, product_sems.at[0, index]).wait()
         pltpu.make_async_copy(far.at[index], far.at[index], product_sems.at[1, index]).wait()
 
     @pl.when(c < chan - 1)
@@ -401,8 +414,8 @@
     feeds = blk * 8
     per, width = N1 // blk, HALF // chan
     chunks = min(per, 2)
-    rows = 2 * width * per // chunks
-    twiddle, high, low = tables()
+    held = per // chunks
+    twiddle, table = tables()
     dma = pltpu.SemaphoreType.DMA
     any_place = pl.BlockSpec(memory_space=pl.ANY)
     near = (per, half, width * 12, 2 * feeds)
@@ -410,28 +423,31 @@
     mine = pl.pallas_call(
         functools.partial(exchange_kernel, (frames, chan, blk)),
         out_shape=[jax.ShapeDtypeStruct(near, jnp.bfloat16), jax.ShapeDtypeStruct(far, jnp.bfloat16)],
-        in_specs=whole(5),
+        in_specs=whole(4),
         out_specs=[any_place, any_place],
         scratch_shapes=[
             pltpu.VMEM((8, (TAPS - 1) * L), jnp.bfloat16),
             pltpu.VMEM((frames * N1, 8, N2), jnp.float32),
-            pltpu.VMEM((N1, 8 * frames, 2 * N2), jnp.float32),
-            pltpu.VMEM((chunks, parts, rows, 128), jnp.bfloat16),
-            pltpu.VMEM((chunks, parts, rows, 128), jnp.bfloat16),
-            pltpu.VMEM((chunks, parts // 2, rows, 128), jnp.bfloat16),
+            pltpu.VMEM((2 * N1, 4 * frames, 2 * N2), jnp.float32),
+            pltpu.VMEM((1, parts, per * width, 128), jnp.bfloat16),
+            pltpu.VMEM((chunks, parts, held * width, 128), jnp.bfloat16),
+            pltpu.VMEM((1, parts, per * width, 128), jnp.bfloat16),
+            pltpu.VMEM((chunks, parts, held * width, 128), jnp.bfloat16),
+            pltpu.VMEM((1, parts // 2, per * width, 128), jnp.bfloat16),
+            pltpu.VMEM((chunks, parts // 2, held * width, 128), jnp.bfloat16),
             pltpu.VMEM((feeds * width, 128), jnp.float32),
             pltpu.VMEM((feeds // 2 * width, 128), jnp.float32),
             pltpu.VMEM(near, jnp.bfloat16),
             pltpu.VMEM(far, jnp.bfloat16),
             dma((2,)),
-            dma((2, chunks)),
-            dma((2, chunks)),
+            dma((2, 1 + chunks)),
+            dma((2, 1 + chunks)),
             dma((2, per)),
             dma((2,)),
         ],
         compiler_params=pltpu.CompilerParams(vmem_limit_bytes=VMEM, collective_id=0, has_side_effects=True),
         name="exchange",
-    )(voltages, fir_taps, jnp.asarray(twiddle), jnp.asarray(high), jnp.asarray(low))
+    )(voltages, fir_taps, jnp.asarray(twiddle), jnp.asarray(table))
     return pl.pallas_call(
         functools.partial(finish_kernel, blk, per, width, feeds),
         out_shape=jax.ShapeDtypeStruct((2, 8, feeds, width * N1), jnp.float32),

time: 56.5 us -> 57.4 us (1.016)
  Pallas kernels: 56.3 us -> 57.2 us
    pallas_call x1, Pallas kernels: 52.6 us -> 53.5 us  [on_device(): pl.pallas_call(functools.partial(exchange_kernel, (frames, chan, blk)), o...]
where the time goes in v4:
time: 57.4 us; the launch traced here: 57.2 us
  Pallas kernels  57.2 us (100%)
    pallas_call x1, Pallas kernels, on_device(): pl.pallas_call(functools.partial(exchange_kernel, (frames, chan, blk)), o...  53.5 us
    pallas_call x1, Pallas kernels, on_device(): pl.pallas_call(functools.partial(finish_kernel, blk, per, width, feeds),...  3.67 us

profile of v4, /device:TPU:0, one launch (start us, length us, event | category | flops | bytes accessed | tf_op | source)
XLA Modules:
  0.0 57.2 jit_solution(5166633458276943385)
XLA Ops:
  0.0 53.5 %exchange.1 = (bf16[4,4,192,128]{3,2,1,0:T(8,128)(2,1)}, bf16[4,4,64,128]{3,2,1,0:T(8,128)(2,1)}) custom-call(bf16[8,65536]{1,0:T(8,128)(2,1)} %volt.1, f32[8,4096]{1,0:T(8,128)} %taps.1, f32[2,32,128]{2,1,0:T(8,128)} %constant.4.clone.twiddle, bf16[256,256]{1,0:T(8,128)(2,1)} %constant.5.clone.table), custom_call_target="tpu_custom_call" | custom-call | tf_op jit(solution)/shard_map/exchange/pallas_call | solution.py:423
  53.5 3.7 %finish.1 = f32[2,8,64,512]{3,2,1,0:T(8,128)} custom-call(bf16[4,4,192,128]{3,2,1,0:T(8,128)(2,1)} %get-tuple-element.7.near, bf16[4,4,64,128]{3,2,1,0:T(8,128)(2,1)} %get-tuple-element.8.far), custom_call_target="tpu_custom_call" | custom-call | tf_op jit(solution)/shard_map/finish/pallas_call | solution.py:451

commit v5 on v4

--- a/solution.py
+++ b/solution.py
@@ -117,7 +117,7 @@
     both = lax.dot_general(table[...], zh, contract, preferred_element_type=jnp.float32)
     rest = lax.dot_general(table[2 * HALF :], zl, contract, preferred_element_type=jnp.float32)
     out = both[2 * HALF :] + (both[: 2 * HALF] + rest)
-    return [value.astype(jnp.bfloat16) for value in join(out[:HALF], out[HALF:], 64)]
+    return [value.astype(jnp.bfloat16) for value in swap_halves(out[:HALF], out[HALF:])]
 
 
 def regroup(groups, lane):
@@ -139,7 +139,7 @@
 def gather_feeds(get, blk, chan, width, place, grouped):
     lane = lax.broadcasted_iota(jnp.int32, (width, 128), 1)
 
-    @pl.loop(0, blk)
+    @pl.loop(0, blk, unroll=blk <= 8)
     def _(b):
         arrays = [get(c, b, part).astype(jnp.float32) for part in range(2) for c in range(chan)]
         for feed, value in enumerate(regroup(arrays, lane)):
@@ -159,43 +159,92 @@
     return lax.dot_general(left, right, (((1,), (1,)), ((), ())), preferred_element_type=jnp.float32)
 
 
-def paired(lefts, rights):
-    zero = jnp.zeros_like(rights[0])
-    right = jnp.concatenate(
-        [jnp.concatenate([rights[0], zero], axis=1), jnp.concatenate([zero, rights[1]], axis=1)], axis=0
-    )
-    return product(jnp.concatenate(lefts, axis=1), right)
+def paired(lefts, rights, order):
+    rows = []
+    for part in range(2):
+        for one in order:
+            zero = jnp.zeros_like(rights[one][part])
+            rows.append(jnp.concatenate([rights[0][part] if one == 0 else zero, rights[1][part] if one else zero], axis=1))
+    return product(jnp.concatenate(lefts, axis=1), jnp.concatenate(rows, axis=0))
+
+
+def quad_by_channel(grouped, nearby, quad, feeds, width):
+    near_feeds = feeds // 2
+    full_rows, far_rows, own_rows = [], [], []
+    for pair in range(2):
+        lefts, rights, own_lefts, own_rights, full = [], [], [], [], []
+        for one in range(2):
+            ch = quad * 4 + pair * 2 + one
+            value, other = sides(grouped, ch, feeds, width)
+            full.append(product(value[:near_feeds], jnp.concatenate([value, other], axis=0)))
+            lefts.append(value[near_feeds:])
+            rights.append((value[:near_feeds], other[:near_feeds]))
+            value, other = sides(nearby, ch, near_feeds, width)
+            own_lefts.append(value)
+            own_rights.append((value, other))
+        full_rows.append(full)
+        far_rows.append(paired(lefts, rights, (1, 0)))
+        own_rows.append(paired(own_lefts, own_rights, (0, 1)))
+    return full_rows, far_rows, own_rows
+
+
+def square(value):
+    turned = value.T
+    other = jnp.concatenate([-turned[64:], turned[:64]], axis=0)
+    right = jnp.concatenate([turned, other], axis=1).astype(jnp.bfloat16)
+    out = jnp.dot(value.astype(jnp.bfloat16), right, preferred_element_type=jnp.float32)
+    return out[:, :128], out[:, 128:]
+
+
+def quad_of_64(grouped, nearby, quad, width):
+    lane = lax.broadcasted_iota(jnp.int32, (32, 128), 1)
+    low, first, third = lane < 64, lane < 32, lane < 96
+
+    def roll(value, shift):
+        return pltpu.roll(value, shift, 1)
+
+    full_rows, far_rows = [], []
+    for pair in range(2):
+        ch = quad * 4 + pair * 2
+        value = jnp.concatenate([grouped[pl.ds(ch + one, 64, stride=width), :] for one in range(2)], axis=0)
+        re, im = square(value)
+        full_rows.append(
+            [
+                jnp.where(low, re[:32], roll(im[:32], 64)),
+                jnp.where(low, roll(re[64:96], 64), im[64:96]),
+            ]
+        )
+        far_rows.append(
+            jnp.where(
+                low,
+                jnp.where(first, roll(re[96:], 64), roll(re[32:64], 32)),
+                jnp.where(third, im[96:], roll(im[32:64], 96)),
+            )
+        )
+    value = jnp.concatenate([nearby[pl.ds(quad * 4 + one, 32, stride=width), :] for one in range(4)], axis=0)
+    re, im = square(value)
+    own_rows = [
+        jnp.where(low, jnp.where(first, re[:32], re[32:64]), roll(jnp.where(first, im[:32], im[32:64]), 64)),
+        jnp.where(low, roll(jnp.where(third, re[64:96], re[96:]), 64), jnp.where(third, im[64:96], im[96:])),
+    ]
+    return full_rows, far_rows, own_rows
 
 
 def correlate(grouped, nearby, half, width, spectra_count, near, far):
-    near_feeds = half * 8
-    feeds = 2 * near_feeds
+    feeds = 16 * half
     scale = 1.0 / spectra_count
 
-    @pl.loop(0, width // 4)
+    @pl.loop(0, width // 4, unroll=True)
     def _(quad):
-        far_rows, own_rows, full_rows = [], [], []
-        for pair in range(2):
-            lefts, rights, own_lefts, own_rights, full = [], [], [], [], []
-            for one in range(2):
-                ch = quad * 4 + pair * 2 + one
-                value, other = sides(grouped, ch, feeds, width)
-                right = jnp.concatenate([value[:near_feeds], other[:near_feeds]], axis=0)
-                rest = jnp.concatenate([value[near_feeds:], other[near_feeds:]], axis=0)
-                full.append(product(value[:near_feeds], jnp.concatenate([right, rest], axis=0)) * scale)
-                lefts.append(value[near_feeds:])
-                rights.append(right)
-                value, other = sides(nearby, ch, near_feeds, width)
-                own_lefts.append(value)
-                own_rights.append(jnp.concatenate([value, other], axis=0))
-            full_rows.append(full)
-            far_rows.append(paired(lefts, rights) * scale)
-            own_rows.append(paired(own_lefts, own_rights) * scale)
+        if feeds == 64:
+            full_rows, far_rows, own_rows = quad_of_64(grouped, nearby, quad, width)
+        else:
+            full_rows, far_rows, own_rows = quad_by_channel(grouped, nearby, quad, feeds, width)
         for b in range(half):
             cut = slice(b * 8, b * 8 + 8)
 
             def put(ref, row, first, second):
-                rows = jnp.concatenate([first[cut], second[cut]], axis=0)
+                rows = jnp.concatenate([first[cut], second[cut]], axis=0) * scale
                 ref[b, pl.ds(pl.multiple_of(row, 16), 16), :] = rows.astype(jnp.bfloat16)
 
             for pair in range(2):
@@ -355,17 +404,26 @@
         halo_copy.wait_send()
 
 
-def join(first, second, feeds):
-    if feeds % 128 == 0:
+def swap_halves(first, second):
+    low_side = lax.broadcasted_iota(jnp.int32, first.shape, 1) < 64
+    return [
+        jnp.where(low_side, first, pltpu.roll(second, 64, 1)),
+        jnp.where(low_side, pltpu.roll(first, 64, 1), second),
+    ]
+
+
+def join(own, other, feeds):
+    count = feeds // 2
+    if count % 128 == 0:
+        cuts = [slice(at, at + count) for at in range(0, 2 * feeds, count)]
         return [
-            jnp.concatenate([first[:, cut], second[:, cut]], axis=1)
-            for cut in (slice(0, feeds), slice(feeds, 2 * feeds))
+            jnp.concatenate([own[:, cuts[0]], other[:, cuts[1]], own[:, cuts[2]], other[:, cuts[3]]], axis=1),
+            jnp.concatenate([own[:, cuts[1]], other[:, cuts[0]], own[:, cuts[3]], other[:, cuts[2]]], axis=1),
         ]
-    lane = lax.broadcasted_iota(jnp.int32, first.shape, 1)
-    low_side = lane < feeds
+    even = lax.broadcasted_iota(jnp.int32, own.shape, 1) // count % 2 == 0
     return [
-        jnp.where(low_side, first, pltpu.roll(second, feeds, 1)),
-        jnp.where(low_side, pltpu.roll(first, feeds, 1), second),
+        jnp.where(even, own, other),
+        jnp.where(even, pltpu.roll(own, 2 * feeds - count, 1), pltpu.roll(other, count, 1)),
     ]
 
 
@@ -398,8 +456,8 @@
             for first in range(0, 2 * feeds, 128):
                 tile = wide[first // 128, pl.ds(block * 8 + i, 128, stride=8), :].T
                 for at in range(0, 128, piece):
-                    which, rest = divmod(first + at, feeds)
-                    part, j = divmod(rest, count)
+                    part, rest = divmod(first + at, feeds)
+                    which, j = divmod(rest, count)
                     start = (side if which == 0 else 1 - side) * count + j
                     out[part, i, pl.ds(pl.multiple_of(start, piece), piece), pl.ds(block, 128)] = tile[at : at + piece]
 

time: 57.4 us -> 53 us (0.923)
  Pallas kernels: 57.2 us -> 52.9 us
    pallas_call x1, Pallas kernels: 53.5 us -> 49.2 us  [on_device(): pl.pallas_call(functools.partial(exchange_kernel, (frames, chan, blk)), o...]
where the time goes in v5:
time: 53 us; the launch traced here: 52.9 us
  Pallas kernels  52.9 us (100%)
    pallas_call x1, Pallas kernels, on_device(): pl.pallas_call(functools.partial(exchange_kernel, (frames, chan, blk)), o...  49.2 us
    pallas_call x1, Pallas kernels, on_device(): pl.pallas_call(functools.partial(finish_kernel, blk, per, width, feeds),...  3.7 us

profile of v5, /device:TPU:0, one launch (start us, length us, event | category | flops | bytes accessed | tf_op | source)
XLA Modules:
  0.0 52.9 jit_solution(17971833008533550838)
XLA Ops:
  0.0 49.2 %exchange.1 = (bf16[4,4,192,128]{3,2,1,0:T(8,128)(2,1)}, bf16[4,4,64,128]{3,2,1,0:T(8,128)(2,1)}) custom-call(bf16[8,65536]{1,0:T(8,128)(2,1)} %volt.1, f32[8,4096]{1,0:T(8,128)} %taps.1, f32[2,32,128]{2,1,0:T(8,128)} %constant.4.clone.twiddle, bf16[256,256]{1,0:T(8,128)(2,1)} %constant.5.clone.table), custom_call_target="tpu_custom_call" | custom-call | tf_op jit(solution)/shard_map/exchange/pallas_call | solution.py:481
  49.2 3.7 %finish.1 = f32[2,8,64,512]{3,2,1,0:T(8,128)} custom-call(bf16[4,4,192,128]{3,2,1,0:T(8,128)(2,1)} %get-tuple-element.7.near, bf16[4,4,64,128]{3,2,1,0:T(8,128)(2,1)} %get-tuple-element.8.far), custom_call_target="tpu_custom_call" | custom-call | tf_op jit(solution)/shard_map/finish/pallas_call | solution.py:509

commit v6 on v5

--- a/solution.py
+++ b/solution.py
@@ -136,14 +136,14 @@
     return groups
 
 
-def gather_feeds(get, blk, chan, width, place, grouped):
+def gather_feeds(get, count, chan, width, start, grouped):
     lane = lax.broadcasted_iota(jnp.int32, (width, 128), 1)
 
-    @pl.loop(0, blk, unroll=blk <= 8)
-    def _(b):
-        arrays = [get(c, b, part).astype(jnp.float32) for part in range(2) for c in range(chan)]
+    @pl.loop(0, count, unroll=count <= 8)
+    def _(at):
+        arrays = [get(c, at, part).astype(jnp.float32) for part in range(2) for c in range(chan)]
         for feed, value in enumerate(regroup(arrays, lane)):
-            row = pl.multiple_of((place(b) * 8 + feed) * width, width)
+            row = pl.multiple_of(((start + at) * 8 + feed) * width, width)
             grouped[pl.ds(row, width), :] = value
 
 
@@ -255,14 +255,15 @@
 
 def exchange_kernel(
     sizes, volt, taps, twiddle, table, out_near, out_far,
-    halo, filtered, turned, sent_late, sent, seen_late, seen, near_late, seen_near, grouped, nearby, near, far,
+    halo, filtered, turned, to_far_late, to_far, to_near_late, to_near,
+    from_far_late, from_far, from_near_late, from_near, grouped, nearby, near, far,
     halo_sems, send_sems, seen_sems, product_sems, out_sems,
 ):
     frames, chan, blk = sizes
     parts, half = chan * blk, blk // 2
     width = HALF // chan
     per = N1 // blk
-    chunks, held = sent.shape[0], per // sent.shape[0]
+    chunks, held = to_far.shape[0], per // to_far.shape[0]
     c, b = lax.axis_index("chan"), lax.axis_index("blk")
     side, spot = lax.div(b, half), lax.rem(b, half)
     barrier = pltpu.get_barrier_semaphore()
@@ -291,39 +292,38 @@
     def _():
         halo[...] = jnp.zeros_like(halo)
 
-    def send(part, q, slot, held, sent, seen, seen_near):
+    def send(part, q, slot, held, to_far, to_near, from_far, from_near):
+        rows = held * width
+
         @pl.loop(0, half)
         def _(t):
             at = lax.rem(spot + 1 + t, half)
             near_b, far_b = side * half + at, (1 - side) * half + at
-            for to_b in (far_b, near_b):
+            for to_b, refs in ((far_b, ((to_far, 0), (to_near, rows))), (near_b, ((to_near, 0),))):
                 base = part * N1 + to_b * per + q * held
                 for first in range(0, held, 2):
                     second = min(first + 1, held - 1)
                     values = second_stage(turned, base + first, base + second, table)
                     for kk in range(first, second + 1):
                         for to_c in range(chan):
-                            rows = pl.ds(kk * width, width)
-                            sent[q, to_c * blk + to_b, rows, :] = values[kk - first][to_c * width : (to_c + 1) * width]
+                            value = values[kk - first][to_c * width : (to_c + 1) * width]
+                            for ref, start in refs:
+                                ref[q, to_c * half + at, pl.ds(start + kk * width, width), :] = value
                 if to_b is far_b:
                     for u in range(chan):
                         to_c = lax.rem(c + u, chan)
-                        block = sent.at[q, to_c * blk + far_b]
-                        dst = seen.at[q, c * blk + b]
+                        block = to_far.at[q, to_c * half + at]
+                        dst = from_far.at[q, c * half + spot]
                         remote(block, dst, send_sems.at[0, slot], seen_sems.at[0, slot], to_c, far_b).start()
             for u in range(chan):
                 to_c = lax.rem(c + u, chan)
-                for kind, to_b, dst in (
-                    (0, near_b, seen.at[q, c * blk + b]),
-                    (1, far_b, seen_near.at[q, c * half + spot]),
-                ):
-                    block = sent.at[q, to_c * blk + to_b]
-                    copy = remote(block, dst, send_sems.at[kind, slot], seen_sems.at[kind, slot], to_c, near_b)
-                    if u == 0:
-                        pl.when(near_b != b)(copy.start)
-                        pl.when(near_b == b)(pltpu.make_async_copy(block, dst, seen_sems.at[kind, slot]).start)
-                    else:
-                        copy.start()
+                block, dst = to_near.at[q, to_c * half + at], from_near.at[q, c * half + spot]
+                copy = remote(block, dst, send_sems.at[1, slot], seen_sems.at[1, slot], to_c, near_b)
+                if u == 0:
+                    pl.when(at != spot)(copy.start)
+                    pl.when(at == spot)(pltpu.make_async_copy(block, dst, seen_sems.at[1, slot]).start)
+                else:
+                    copy.start()
 
     count = frames // 2
     fir_stage(volt, halo, taps, filtered, (count, frames))
@@ -336,7 +336,7 @@
         halo_copy.start()
 
     first_stage(filtered, twiddle, turned, 1, count)
-    send(1, 0, 0, per, sent_late, seen_late, near_late)
+    send(1, 0, 0, per, to_far_late, to_near_late, from_far_late, from_near_late)
 
     @pl.when(c > 0)
     def _():
@@ -345,32 +345,31 @@
     fir_stage(volt, halo, taps, filtered, (0, count))
     first_stage(filtered, twiddle, turned, 0, count)
     for q in range(chunks):
-        send(0, q, 1 + q, held, sent, seen, seen_near)
+        send(0, q, 1 + q, held, to_far, to_near, from_far, from_near)
 
     def arrived(ref, kind, q, slot):
         pltpu.make_async_copy(ref.at[q], ref.at[q], seen_sems.at[kind, slot]).wait()
 
-    arrived(seen_late, 0, 0, 0)
-    arrived(near_late, 1, 0, 0)
+    arrived(from_far_late, 0, 0, 0)
+    arrived(from_near_late, 1, 0, 0)
     for q in range(chunks):
-        arrived(seen, 0, q, 1 + q)
-        arrived(seen_near, 1, q, 1 + q)
+        arrived(from_far, 0, q, 1 + q)
+        arrived(from_near, 1, q, 1 + q)
         for kk in range(held):
             index = q * held + kk
 
-            def block(late, early, source, part):
-                if part == 1:
-                    return late[0, source, pl.ds(index * width, width), :]
-                return early[q, source, pl.ds(kk * width, width), :]
-
-            def get(from_c, from_b, part):
-                return block(seen_late, seen, from_c * blk + from_b, part)
-
-            def get_near(from_c, at, part):
-                return block(near_late, seen_near, from_c * half + at, part)
-
-            gather_feeds(get, blk, chan, width, lambda from_b: lax.rem(from_b + side * half, blk), grouped)
-            gather_feeds(get_near, half, chan, width, lambda at: at, nearby)
+            def reader(late, early, second):
+                def get(from_c, at, part):
+                    source = from_c * half + at
+                    if part == 1:
+                        return late[0, source, pl.ds((second * per + index) * width, width), :]
+                    return early[q, source, pl.ds((second * held + kk) * width, width), :]
+
+                return get
+
+            gather_feeds(reader(from_near_late, from_near, 0), half, chan, width, 0, grouped)
+            gather_feeds(reader(from_far_late, from_far, 0), half, chan, width, half, grouped)
+            gather_feeds(reader(from_near_late, from_near, 1), half, chan, width, 0, nearby)
             correlate(grouped, nearby, half, width, frames * chan, near.at[index], far.at[index])
 
             @pl.loop(0, half)
@@ -390,10 +389,11 @@
     pltpu.make_async_copy(out_near, out_near, out_sems.at[0]).wait()
     pltpu.make_async_copy(out_far, out_far, out_sems.at[1]).wait()
     for slot in range(1 + chunks):
-        ref, q = (sent_late, 0) if slot == 0 else (sent, slot - 1)
-        for kind, number in enumerate((parts, chan * half)):
-            piece = ref.at[q, pl.ds(0, number - 1)]
-            pltpu.make_async_copy(piece, piece, send_sems.at[kind, slot]).wait()
+        q = max(slot - 1, 0)
+        piece = (to_far if slot else to_far_late).at[q]
+        pltpu.make_async_copy(piece, piece, send_sems.at[0, slot]).wait()
+        piece = (to_near if slot else to_near_late).at[q, pl.ds(0, chan * half - 1)]
+        pltpu.make_async_copy(piece, piece, send_sems.at[1, slot]).wait()
     for index in range(per):
         piece = near.at[index, pl.ds(0, half - 1)]
         pltpu.make_async_copy(piece, piece, product_sems.at[0, index]).wait()
@@ -436,30 +436,33 @@
         for first in range(0, 2 * feeds, 128):
             wide[first // 128, pl.ds(row, 8), :] = rows[:, first : first + 128]
 
-    @pl.loop(0, half)
-    def _(at):
-        near_b, far_b = side * half + at, (1 - side) * half + at
-        for kk in range(per):
-            value = near[kk, at].astype(jnp.float32)
-            other = far[kk, at].astype(jnp.float32)
-            for k2 in range(width):
-                put(k2, near_b * per + kk, value[k2 * 8 : k2 * 8 + 8])
-            for pair in range(width // 2):
-                own = value[(width + pair) * 8 : (width + pair) * 8 + 8]
-                for one, rows in enumerate(join(own, other[pair * 8 : pair * 8 + 8], feeds)):
-                    put(2 * pair + one, far_b * per + kk, rows)
+    i = pl.program_id(0)
+
+    @pl.when(i == 0)
+    def _():
+        @pl.loop(0, half)
+        def _(at):
+            near_b, far_b = side * half + at, (1 - side) * half + at
+            for kk in range(per):
+                value = near[kk, at].astype(jnp.float32)
+                other = far[kk, at].astype(jnp.float32)
+                for k2 in range(width):
+                    put(k2, near_b * per + kk, value[k2 * 8 : k2 * 8 + 8])
+                for pair in range(width // 2):
+                    own = value[(width + pair) * 8 : (width + pair) * 8 + 8]
+                    for one, rows in enumerate(join(own, other[pair * 8 : pair * 8 + 8], feeds)):
+                        put(2 * pair + one, far_b * per + kk, rows)
 
     count = feeds // 2
     piece = min(count, 128)
-    for i in range(8):
-        for block in range(0, width * N1, 128):
-            for first in range(0, 2 * feeds, 128):
-                tile = wide[first // 128, pl.ds(block * 8 + i, 128, stride=8), :].T
-                for at in range(0, 128, piece):
-                    part, rest = divmod(first + at, feeds)
-                    which, j = divmod(rest, count)
-                    start = (side if which == 0 else 1 - side) * count + j
-                    out[part, i, pl.ds(pl.multiple_of(start, piece), piece), pl.ds(block, 128)] = tile[at : at + piece]
+    for block in range(0, width * N1, 128):
+        for first in range(0, 2 * feeds, 128):
+            tile = wide[first // 128, pl.ds(block * 8 + i, 128, stride=8), :].T
+            for at in range(0, 128, piece):
+                part, rest = divmod(first + at, feeds)
+                which, j = divmod(rest, count)
+                start = (side if which == 0 else 1 - side) * count + j
+                out[part, 0, pl.ds(pl.multiple_of(start, piece), piece), pl.ds(block, 128)] = tile[at : at + piece]
 
 
 def whole(count):
@@ -471,10 +474,14 @@
     parts, half = chan * blk, blk // 2
     feeds = blk * 8
     per, width = N1 // blk, HALF // chan
-    chunks = min(per, 2)
-    held = per // chunks
+    chunks = per
     twiddle, table = tables()
     dma = pltpu.SemaphoreType.DMA
+    blocks = [
+        pltpu.VMEM((pieces, parts // 2, sets * width * per // pieces, 128), jnp.bfloat16)
+        for sets in (1, 2)
+        for pieces in (1, chunks)
+    ]
     any_place = pl.BlockSpec(memory_space=pl.ANY)
     near = (per, half, width * 12, 2 * feeds)
     far = (per, half, width * 4, 2 * feeds)
@@ -487,12 +494,8 @@
             pltpu.VMEM((8, (TAPS - 1) * L), jnp.bfloat16),
             pltpu.VMEM((frames * N1, 8, N2), jnp.float32),
             pltpu.VMEM((2 * N1, 4 * frames, 2 * N2), jnp.float32),
-            pltpu.VMEM((1, parts, per * width, 128), jnp.bfloat16),
-            pltpu.VMEM((chunks, parts, held * width, 128), jnp.bfloat16),
-            pltpu.VMEM((1, parts, per * width, 128), jnp.bfloat16),
-            pltpu.VMEM((chunks, parts, held * width, 128), jnp.bfloat16),
-            pltpu.VMEM((1, parts // 2, per * width, 128), jnp.bfloat16),
-            pltpu.VMEM((chunks, parts // 2, held * width, 128), jnp.bfloat16),
+            *blocks,
+            *blocks,
             pltpu.VMEM((feeds * width, 128), jnp.float32),
             pltpu.VMEM((feeds // 2 * width, 128), jnp.float32),
             pltpu.VMEM(near, jnp.bfloat16),
@@ -509,8 +512,9 @@
     return pl.pallas_call(
         functools.partial(finish_kernel, blk, per, width, feeds),
         out_shape=jax.ShapeDtypeStruct((2, 8, feeds, width * N1), jnp.float32),
+        grid=(8,),
         in_specs=whole(2),
-        out_specs=whole(1)[0],
+        out_specs=pl.BlockSpec((2, 1, feeds, width * N1), lambda i: (0, i, 0, 0)),
         scratch_shapes=[pltpu.VMEM((feeds // 64, width * N1 * 8, 128), jnp.float32)],
         compiler_params=pltpu.CompilerParams(vmem_limit_bytes=VMEM),
         name="finish",

time: 53 us -> 53.1 us (level)
    pallas_call x1, Pallas kernels: 3.7 us -> 5.31 us  [on_device(): pl.pallas_call(functools.partial(finish_kernel, blk, per, width, feeds),...]
    pallas_call x1, Pallas kernels: 49.2 us -> 47.7 us  [on_device(): pl.pallas_call(functools.partial(exchange_kernel, (frames, chan, blk)), o...]
where the time goes in v6:
time: 53.1 us; the launch traced here: 53 us
  Pallas kernels  53 us (100%)
    pallas_call x1, Pallas kernels, on_device(): pl.pallas_call(functools.partial(exchange_kernel, (frames, chan, blk)), o...  47.7 us
    pallas_call x1, Pallas kernels, on_device(): pl.pallas_call(functools.partial(finish_kernel, blk, per, width, feeds),...  5.31 us

profile of v6, /device:TPU:0, one launch (start us, length us, event | category | flops | bytes accessed | tf_op | source)
XLA Modules:
  0.0 53.0 jit_solution(388947973859405426)
XLA Ops:
  0.0 47.7 %exchange.1 = (bf16[4,4,192,128]{3,2,1,0:T(8,128)(2,1)}, bf16[4,4,64,128]{3,2,1,0:T(8,128)(2,1)}) custom-call(bf16[8,65536]{1,0:T(8,128)(2,1)} %volt.1, f32[8,4096]{1,0:T(8,128)} %taps.1, f32[2,32,128]{2,1,0:T(8,128)} %constant.4.clone.twiddle, bf16[256,256]{1,0:T(8,128)(2,1)} %constant.5.clone.table), custom_call_target="tpu_custom_call" | custom-call | tf_op jit(solution)/shard_map/exchange/pallas_call | solution.py:488
  47.7 5.3 %finish.1 = f32[2,8,64,512]{3,2,1,0:T(8,128)} custom-call(bf16[4,4,192,128]{3,2,1,0:T(8,128)(2,1)} %get-tuple-element.7.near, bf16[4,4,64,128]{3,2,1,0:T(8,128)(2,1)} %get-tuple-element.8.far), custom_call_target="tpu_custom_call" | custom-call | tf_op jit(solution)/shard_map/finish/pallas_call | solution.py:512

commit v7 on v6

--- a/solution.py
+++ b/solution.py
@@ -299,16 +299,17 @@
         def _(t):
             at = lax.rem(spot + 1 + t, half)
             near_b, far_b = side * half + at, (1 - side) * half + at
-            for to_b, refs in ((far_b, ((to_far, 0), (to_near, rows))), (near_b, ((to_near, 0),))):
-                base = part * N1 + to_b * per + q * held
-                for first in range(0, held, 2):
-                    second = min(first + 1, held - 1)
-                    values = second_stage(turned, base + first, base + second, table)
-                    for kk in range(first, second + 1):
-                        for to_c in range(chan):
-                            value = values[kk - first][to_c * width : (to_c + 1) * width]
-                            for ref, start in refs:
-                                ref[q, to_c * half + at, pl.ds(start + kk * width, width), :] = value
+            bases = [part * N1 + to_b * per + q * held for to_b in (far_b, near_b)]
+            single = second_stage(turned, *bases, table) if held == 1 else None
+            for one, (to_b, refs) in enumerate(((far_b, ((to_far, 0), (to_near, rows))), (near_b, ((to_near, 0),)))):
+                values = [single[one]] if held == 1 else []
+                for first in range(0, held - 1, 2):
+                    values += second_stage(turned, bases[one] + first, bases[one] + first + 1, table)
+                for kk in range(held):
+                    for to_c in range(chan):
+                        value = values[kk][to_c * width : (to_c + 1) * width]
+                        for ref, start in refs:
+                            ref[q, to_c * half + at, pl.ds(start + kk * width, width), :] = value
                 if to_b is far_b:
                     for u in range(chan):
                         to_c = lax.rem(c + u, chan)
@@ -427,7 +428,7 @@
     ]
 
 
-def finish_kernel(blk, per, width, feeds, near, far, out, wide):
+def finish_kernel(blk, per, width, feeds, near, far, out, wide, built, sems):
     half = blk // 2
     side = lax.div(lax.axis_index("blk"), half)
 
@@ -436,33 +437,37 @@
         for first in range(0, 2 * feeds, 128):
             wide[first // 128, pl.ds(row, 8), :] = rows[:, first : first + 128]
 
-    i = pl.program_id(0)
-
-    @pl.when(i == 0)
-    def _():
-        @pl.loop(0, half)
-        def _(at):
-            near_b, far_b = side * half + at, (1 - side) * half + at
-            for kk in range(per):
-                value = near[kk, at].astype(jnp.float32)
-                other = far[kk, at].astype(jnp.float32)
-                for k2 in range(width):
-                    put(k2, near_b * per + kk, value[k2 * 8 : k2 * 8 + 8])
-                for pair in range(width // 2):
-                    own = value[(width + pair) * 8 : (width + pair) * 8 + 8]
-                    for one, rows in enumerate(join(own, other[pair * 8 : pair * 8 + 8], feeds)):
-                        put(2 * pair + one, far_b * per + kk, rows)
+    @pl.loop(0, half)
+    def _(at):
+        near_b, far_b = side * half + at, (1 - side) * half + at
+        for kk in range(per):
+            value = near[kk, at].astype(jnp.float32)
+            other = far[kk, at].astype(jnp.float32)
+            for k2 in range(width):
+                put(k2, near_b * per + kk, value[k2 * 8 : k2 * 8 + 8])
+            for pair in range(width // 2):
+                own = value[(width + pair) * 8 : (width + pair) * 8 + 8]
+                for one, rows in enumerate(join(own, other[pair * 8 : pair * 8 + 8], feeds)):
+                    put(2 * pair + one, far_b * per + kk, rows)
 
     count = feeds // 2
     piece = min(count, 128)
-    for block in range(0, width * N1, 128):
-        for first in range(0, 2 * feeds, 128):
-            tile = wide[first // 128, pl.ds(block * 8 + i, 128, stride=8), :].T
-            for at in range(0, 128, piece):
-                part, rest = divmod(first + at, feeds)
-                which, j = divmod(rest, count)
-                start = (side if which == 0 else 1 - side) * count + j
-                out[part, 0, pl.ds(pl.multiple_of(start, piece), piece), pl.ds(block, 128)] = tile[at : at + piece]
+    copies = []
+    for i in range(8):
+        for block in range(0, width * N1, 128):
+            for first in range(0, 2 * feeds, 128):
+                tile = wide[first // 128, pl.ds(block * 8 + i, 128, stride=8), :].T
+                for at in range(0, 128, piece):
+                    part, rest = divmod(first + at, feeds)
+                    which, j = divmod(rest, count)
+                    start = (side if which == 0 else 1 - side) * count + j
+                    rows = pl.ds(pl.multiple_of(start, piece), piece)
+                    built[i, part, rows, pl.ds(block, 128)] = tile[at : at + piece]
+        for part in range(2):
+            copies.append(pltpu.make_async_copy(built.at[i, part], out.at[part, i], sems.at[i, part]))
+            copies[-1].start()
+    for copy in copies:
+        copy.wait()
 
 
 def whole(count):
@@ -512,10 +517,13 @@
     return pl.pallas_call(
         functools.partial(finish_kernel, blk, per, width, feeds),
         out_shape=jax.ShapeDtypeStruct((2, 8, feeds, width * N1), jnp.float32),
-        grid=(8,),
         in_specs=whole(2),
-        out_specs=pl.BlockSpec((2, 1, feeds, width * N1), lambda i: (0, i, 0, 0)),
-        scratch_shapes=[pltpu.VMEM((feeds // 64, width * N1 * 8, 128), jnp.float32)],
+        out_specs=any_place,
+        scratch_shapes=[
+            pltpu.VMEM((feeds // 64, width * N1 * 8, 128), jnp.float32),
+            pltpu.VMEM((8, 2, feeds, width * N1), jnp.float32),
+            dma((8, 2)),
+        ],
         compiler_params=pltpu.CompilerParams(vmem_limit_bytes=VMEM),
         name="finish",
     )(*mine)

time: 53.1 us -> 51.4 us (0.968)
  Pallas kernels: 53 us -> 51.3 us
    pallas_call x1, Pallas kernels: 5.31 us -> 3.31 us  [on_device(): pl.pallas_call(functools.partial(finish_kernel, blk, per, width, feeds),...]
where the time goes in v7:
time: 51.4 us; the launch traced here: 51.3 us
  Pallas kernels  51.3 us (100%)
    pallas_call x1, Pallas kernels, on_device(): pl.pallas_call(functools.partial(exchange_kernel, (frames, chan, blk)), o...  48 us
    pallas_call x1, Pallas kernels, on_device(): pl.pallas_call(functools.partial(finish_kernel, blk, per, width, feeds),...  3.31 us

profile of v7, /device:TPU:0, one launch (start us, length us, event | category | flops | bytes accessed | tf_op | source)
XLA Modules:
  0.0 51.3 jit_solution(12499928484100472104)
XLA Ops:
  0.0 48.0 %exchange.1 = (bf16[4,4,192,128]{3,2,1,0:T(8,128)(2,1)}, bf16[4,4,64,128]{3,2,1,0:T(8,128)(2,1)}) custom-call(bf16[8,65536]{1,0:T(8,128)(2,1)} %volt.1, f32[8,4096]{1,0:T(8,128)} %taps.1, f32[2,32,128]{2,1,0:T(8,128)} %constant.4.clone.twiddle, bf16[256,256]{1,0:T(8,128)(2,1)} %constant.5.clone.table), custom_call_target="tpu_custom_call" | custom-call | tf_op jit(solution)/shard_map/exchange/pallas_call | solution.py:493
  48.0 3.3 %finish.1 = f32[2,8,64,512]{3,2,1,0:T(8,128)} custom-call(bf16[4,4,192,128]{3,2,1,0:T(8,128)(2,1)} %get-tuple-element.7.near, bf16[4,4,64,128]{3,2,1,0:T(8,128)(2,1)} %get-tuple-element.8.far), custom_call_target="tpu_custom_call" | custom-call | tf_op jit(solution)/shard_map/finish/pallas_call | solution.py:517

commit v8 on v7

--- a/solution.py
+++ b/solution.py
@@ -479,7 +479,7 @@
     parts, half = chan * blk, blk // 2
     feeds = blk * 8
     per, width = N1 // blk, HALF // chan
-    chunks = per
+    chunks = min(per, 2)
     twiddle, table = tables()
     dma = pltpu.SemaphoreType.DMA
     blocks = [

time: 51.4 us -> 52.8 us (1.027)
  Pallas kernels: 51.3 us -> 52.6 us
    pallas_call x1, Pallas kernels: 48 us -> 49.3 us  [on_device(): pl.pallas_call(functools.partial(exchange_kernel, (frames, chan, blk)), o...]
where the time goes in v8:
time: 52.8 us; the launch traced here: 52.6 us
  Pallas kernels  52.6 us (100%)
    pallas_call x1, Pallas kernels, on_device(): pl.pallas_call(functools.partial(exchange_kernel, (frames, chan, blk)), o...  49.3 us
    pallas_call x1, Pallas kernels, on_device(): pl.pallas_call(functools.partial(finish_kernel, blk, per, width, feeds),...  3.31 us

profile of v8, /device:TPU:0, one launch (start us, length us, event | category | flops | bytes accessed | tf_op | source)
XLA Modules:
  0.0 52.6 jit_solution(14170373185878233422)
XLA Ops:
  0.0 49.3 %exchange.1 = (bf16[4,4,192,128]{3,2,1,0:T(8,128)(2,1)}, bf16[4,4,64,128]{3,2,1,0:T(8,128)(2,1)}) custom-call(bf16[8,65536]{1,0:T(8,128)(2,1)} %volt.1, f32[8,4096]{1,0:T(8,128)} %taps.1, f32[2,32,128]{2,1,0:T(8,128)} %constant.4.clone.twiddle, bf16[256,256]{1,0:T(8,128)(2,1)} %constant.5.clone.table), custom_call_target="tpu_custom_call" | custom-call | tf_op jit(solution)/shard_map/exchange/pallas_call | solution.py:493
  49.3 3.3 %finish.1 = f32[2,8,64,512]{3,2,1,0:T(8,128)} custom-call(bf16[4,4,192,128]{3,2,1,0:T(8,128)(2,1)} %get-tuple-element.7.near, bf16[4,4,64,128]{3,2,1,0:T(8,128)(2,1)} %get-tuple-element.8.far), custom_call_target="tpu_custom_call" | custom-call | tf_op jit(solution)/shard_map/finish/pallas_call | solution.py:517

commit v9 on v7

--- a/solution.py
+++ b/solution.py
@@ -67,7 +67,7 @@
 def fir_stage(volt, halo, taps, filtered, frames):
     first, end = frames
 
-    @pl.loop(0, N1)
+    @pl.loop(0, N1, unroll=2)
     def _(n1):
         lane = pl.multiple_of(n1 * N2, N2)
         weights = [jnp.broadcast_to(taps[t : t + 1, pl.ds(lane, N2)], (8, N2)) for t in range(TAPS)]

time: 51.4 us -> 51.5 us (level)
  no operation moved by 1% of the time
where the time goes in v9:
time: 51.5 us; the launch traced here: 51.3 us
  Pallas kernels  51.3 us (100%)
    pallas_call x1, Pallas kernels, on_device(): pl.pallas_call(functools.partial(exchange_kernel, (frames, chan, blk)), o...  48 us
    pallas_call x1, Pallas kernels, on_device(): pl.pallas_call(functools.partial(finish_kernel, blk, per, width, feeds),...  3.31 us

profile of v9, /device:TPU:0, one launch (start us, length us, event | category | flops | bytes accessed | tf_op | source)
XLA Modules:
  0.0 51.3 jit_solution(3971835006336753486)
XLA Ops:
  0.0 48.0 %exchange.1 = (bf16[4,4,192,128]{3,2,1,0:T(8,128)(2,1)}, bf16[4,4,64,128]{3,2,1,0:T(8,128)(2,1)}) custom-call(bf16[8,65536]{1,0:T(8,128)(2,1)} %volt.1, f32[8,4096]{1,0:T(8,128)} %taps.1, f32[2,32,128]{2,1,0:T(8,128)} %constant.4.clone.twiddle, bf16[256,256]{1,0:T(8,128)(2,1)} %constant.5.clone.table), custom_call_target="tpu_custom_call" | custom-call | tf_op jit(solution)/shard_map/exchange/pallas_call | solution.py:493
  48.0 3.3 %finish.1 = f32[2,8,64,512]{3,2,1,0:T(8,128)} custom-call(bf16[4,4,192,128]{3,2,1,0:T(8,128)(2,1)} %get-tuple-element.7.near, bf16[4,4,64,128]{3,2,1,0:T(8,128)(2,1)} %get-tuple-element.8.far), custom_call_target="tpu_custom_call" | custom-call | tf_op jit(solution)/shard_map/finish/pallas_call | solution.py:517
